TPU v7x, 32 devices: a whole 2x2x4 slice. The times are simulated.
32 devices in a mesh: context: 4 (over z), channel: 4 (over y, core), dp: 2 (over x).
Axes of the slice: x: 2, y: 2, z: 4, core: 2. Of those that a mesh axis runs over, the one named last changes fastest.
Arguments:
- features: bfloat16 [2, 2048, 3, 2048], P('dp', 'context', None, 'channel'), may hold values from -6 to 6
- doc_start: int32 [2, 4], P('dp'), may hold values 0 or 1
- short_taps: float32 [3, 3, 2048], P(None, None, 'channel'), may hold values from -3 to 3
- long_filter: bfloat16 [2048, 2048], P('channel', 'dp'), may hold values from -0.125 to 0.125
- w_out: bfloat16 [2048, 2048], P('channel'), may hold values from -0.125 to 0.125
Outputs:
- layer_out: bfloat16 [2, 2048, 2048], P('dp', ('context', 'channel'))
Inputs may be any that keep to these rules, and one draw needn't show every extreme that they name: `doc_start`: block 0 of every sequence begins a document whatever its entry.
All inputs are finite; a program needn't handle non-finite values.
Results may differ from a plain program's by a relative error of at most 0.023.
Values may be sent and summed in bfloat16 or wider, within the bound.
No kernel may reach another device: no remote copies, remote signals or barrier semaphores. Data moves between devices by JAX's collectives and lax.ppermute only.
A program may use at most 64 MiB of HBM per device.

v0:
```python
import functools
import math

import jax
import jax.numpy as jnp
import numpy as np
from jax import lax
from jax.experimental import pallas as pl
from jax.experimental.pallas import tpu as pltpu
from jax.sharding import Mesh
from jax.sharding import PartitionSpec as P

SEGS = 4
LANES = 128
EXTRA = 16
PLACES = 4
PARAMS = pltpu.CompilerParams(vmem_limit_bytes=14 * 1024 * 1024)
HBM = pl.BlockSpec(memory_space=pltpu.HBM)
SMEM = pl.BlockSpec(memory_space=pltpu.SMEM)
VMEM = pl.BlockSpec(memory_space=pltpu.VMEM)


def spectrum_table(block_len):
    width = 2 * block_len
    rows = np.arange(width)[:, None]
    cols = np.arange(block_len)[None, :]
    freq = np.where(rows == block_len, block_len, rows % block_len)
    angle = (freq * cols % width) * (2.0 * math.pi / width)
    return np.where(rows <= block_len, np.cos(angle), -np.sin(angle)).astype(jnp.bfloat16)


def outputs_table(block_len):
    width = 2 * block_len
    outputs = np.arange(block_len)[:, None]
    cols = np.arange(width)[None, :]
    freq = cols % block_len
    angle = (freq * outputs % width) * (2.0 * math.pi / width)
    real_part = np.where(cols == 0, 1.0, 2.0 * np.cos(angle))
    nyquist = np.where(outputs % 2 == 0, 1.0, -1.0)
    imag_part = np.where(cols == block_len, nyquist, -2.0 * np.sin(angle))
    return (np.where(cols < block_len, real_part, imag_part) / width).astype(jnp.bfloat16)


def lane_block(index, lanes):
    return pl.ds(pl.multiple_of(index * lanes, lanes), lanes)


def edge_rows(groups):
    return -(-(8 + 2 * groups) // EXTRA) * EXTRA


def product_kernel(groups, offsets, streams_hbm, taps_hbm, *refs):
    kv, q, taps_ref, ext, sems, taps_sem, q_sem, filter_sem = refs[-8:]
    filter_refs, outs = refs[: -8 - len(offsets)], refs[-8 - len(offsets) : -8]
    n, lanes = kv.shape[2], kv.shape[3]
    me = lax.axis_index("context")

    def started(source, target, sem):
        copy = pltpu.make_async_copy(source, target, sem)
        copy.start()
        return copy

    taps_copy = started(taps_hbm, taps_ref, taps_sem)
    q_copy = started(streams_hbm.at[0, n - EXTRA : n], q, q_sem)
    loads = [
        [
            started(streams_hbm.at[s + 1, :, lane_block(me ^ offset, lanes)], kv.at[i, s], sems.at[i, s])
            for s in range(2)
        ]
        for i, offset in enumerate(offsets)
    ]
    if filter_refs:
        filter_copy = started(filter_refs[0].at[lane_block(me, lanes)], filter_refs[1], filter_sem)
    taps_copy.wait()
    q_copy.wait()
    last = q[...].astype(jnp.float32)[EXTRA - 2 :]
    tails = [last[t : t + 1, g * lanes : (g + 1) * lanes] for t in range(2) for g in range(groups)]
    for i, offset in enumerate(offsets):
        taps = taps_ref[:, :, lane_block(me ^ offset, lanes)]
        smoothed, edges = [], []
        for s in range(2):
            loads[i][s].wait()
            x = kv[i, s].astype(jnp.float32)
            t = [taps[j, s + 1 : s + 2] for j in range(3)]
            ext[8:, :] = x
            ext[0:8, :] = jnp.zeros((8, lanes), jnp.float32)
            smoothed.append(t[0] * x + t[1] * ext[7 : 7 + n, :] + t[2] * ext[6 : 6 + n, :])
            edges += [x[0:2], x[n - 2 : n]]
        outs[i][0:n, :] = (smoothed[0] * smoothed[1]).astype(jnp.bfloat16)
        spare = outs[i].shape[0] - n - 8 - 2 * groups
        edges += tails + ([jnp.zeros((spare, lanes), jnp.float32)] if spare else [])
        outs[i][n:, :] = jnp.concatenate(edges, 0).astype(jnp.bfloat16)
    if filter_refs:
        filter_copy.wait()


def query_kernel(streams_ref, taps_ref, keep_ref, send_ref, q, ext, smooth, sem):
    n = smooth.shape[0]
    load = pltpu.make_async_copy(streams_ref.at[0], q, sem)
    load.start()
    ext[0:8, :] = jnp.zeros((8, ext.shape[1]), jnp.float32)
    load.wait()
    ext[8:, :] = q[...].astype(jnp.float32)
    t = [taps_ref[j, 0:1] for j in range(3)]
    smooth[...] = t[0] * ext[8:, :] + t[1] * ext[7 : 7 + n, :] + t[2] * ext[6 : 6 + n, :]
    rows = n // PLACES
    cy, cc = lax.axis_index("cy"), lax.axis_index("cc")
    for out_ref, core in ((keep_ref, cc), (send_ref, 1 - cc)):
        for at, place in enumerate((1 - cy, cy)):
            first = pl.multiple_of((2 * place + core) * rows, rows)
            out_ref[at] = smooth[pl.ds(first, rows), :].astype(out_ref.dtype)


def document_pairs(groups, lags):
    return [(g, d) for g in range(groups) for d in range(1, min(lags, g + 1))]


def filter_kernel(groups, begin_ref, fwd_ref, *refs):
    taps_refs, (out_ref, masks_ref, held) = refs[:-3], refs[-3:]
    peers = len(taps_refs)
    block_len = fwd_ref.shape[1]
    per = taps_refs[0].shape[1] // block_len
    lags = out_ref.shape[0]
    me = lax.axis_index("dp")
    for k in range(peers):
        owner = lax.rem(me + peers - k, peers)
        for i in range(per):
            held[owner * per + i] = lax.dot_general(
                fwd_ref[...],
                taps_refs[k][:, i * block_len : (i + 1) * block_len],
                (((1,), (1,)), ((), ())),
                preferred_element_type=jnp.float32,
            )
    rows = lax.broadcasted_iota(jnp.int32, (2 * block_len, 1), 0)
    sign = jnp.where(rows % 2 == 0, 1.0, -1.0)
    segs = peers * per
    for d in range(lags):
        total = held[d] if d < segs else None
        if d:
            turned = sign * held[d - 1]
            total = turned if total is None else total + turned
        out_ref[d] = total

    docs = [jnp.int32(1)]
    for g in range(1, groups):
        docs.append(docs[-1] + jnp.where(begin_ref[0, g] == 1, 1, 0))
    group = lax.axis_index("context")
    begins = jnp.where(group == 0, 1, begin_ref[0, group])
    marks = [jnp.where(docs[g] == docs[g - d], 1.0, 0.0) for g, d in document_pairs(groups, lags)]
    marks.append(jnp.where(begins == 1, 0.0, 1.0))
    for at, mark in enumerate(marks):
        masks_ref[at] = jnp.full(masks_ref.shape[1:], mark, jnp.float32)


def gather_kernel(places, *refs):
    ins, (prod_ref, edge_ref) = refs[:-2], refs[-2:]
    block_len = prod_ref.shape[0]
    lanes = ins[0].shape[1]
    me = lax.axis_index("context")
    for offset, piece_ref in zip(places, ins):
        prod_ref[:, lane_block(me ^ offset, lanes)] = piece_ref[0:block_len, :]
        edge_ref[me ^ offset] = piece_ref[block_len:, :].astype(jnp.float32)


def conv_kernel(places, near, masks_ref, far_ref, far_edge_ref, fwd_ref, inv_ref, taps_ref, spec_ref, *refs):
    groups = len(places)
    ins, (cross_ref, added_ref, zed, prod, edge, spec, conv) = refs[:near], refs[near:]
    block_len = prod.shape[0]
    lanes = ins[0].shape[1]
    lags = spec_ref.shape[0]
    me = lax.axis_index("context")
    taps = taps_ref[:, :, lane_block(me, lanes)]
    pairs = document_pairs(groups, lags)
    masks = {pair: masks_ref[at] for at, pair in enumerate(pairs)}

    for offset in places[: groups - near]:
        edge[me ^ offset] = far_edge_ref[me ^ offset]
    for offset, piece_ref in zip(places[groups - near :], ins):
        prod[:, lane_block(me ^ offset, lanes)] = piece_ref[0:block_len, :]
        edge[me ^ offset] = piece_ref[block_len:, :].astype(jnp.float32)
    row16 = lax.broadcasted_iota(jnp.int32, (EXTRA, 1), 0)
    for s in range(1, groups):
        cols = slice(s * lanes, (s + 1) * lanes)
        here, past = edge[s], edge[s - 1]
        first, second = [], []
        for stream, at in ((1, 0), (2, 4)):
            t = [taps[j, stream : stream + 1] for j in range(3)]
            x0, x1 = here[at : at + 1], here[at + 1 : at + 2]
            m2, m1 = past[at + 2 : at + 3], past[at + 3 : at + 4]
            first.append(t[0] * x0 + t[1] * m1 + t[2] * m2)
            second.append(t[0] * x1 + t[1] * x0 + t[2] * m1)
        fixed = jnp.where(row16 == 0, first[0] * first[1], second[0] * second[1])
        old = prod[0:EXTRA, cols].astype(jnp.float32)
        joined = masks[s, 1] > 0.5
        prod[0:EXTRA, cols] = jnp.where((row16 < 2) & joined, fixed, old).astype(jnp.bfloat16)

    def chunk(at):
        lo = slice(at, at + EXTRA)
        hi = slice(at + block_len, at + block_len + EXTRA)
        src = [
            (spec[lo, s * lanes : (s + 1) * lanes], spec[hi, s * lanes : (s + 1) * lanes])
            for s in range(groups)
        ]
        fil = [(spec_ref[d, lo, :], spec_ref[d, hi, :]) for d in range(lags)]
        for g in range(groups):
            re = im = None
            for d in range(min(lags, g + 1)):
                fr, fi = fil[d]
                sr, si = src[g - d]
                pr, pi = fr * sr - fi * si, fr * si + fi * sr
                if at == 0:
                    pr = jnp.where(row16 == 0, fr * sr, pr)
                    pi = jnp.where(row16 == 0, fi * si, pi)
                if d:
                    pr, pi = masks[g, d] * pr, masks[g, d] * pi
                re, im = (pr, pi) if re is None else (re + pr, im + pi)
            zed[lo, g * lanes : (g + 1) * lanes] = re.astype(jnp.bfloat16)
            zed[hi, g * lanes : (g + 1) * lanes] = im.astype(jnp.bfloat16)

    spec[...] = jnp.dot(fwd_ref[...], prod[...], preferred_element_type=jnp.float32)
    for at in range(0, block_len, EXTRA):
        chunk(at)
    invert(1 - lax.axis_index("cy"), 1 - lax.axis_index("cc"), inv_ref, zed, cross_ref, conv)
    past = edge[jnp.maximum(me, 1) - 1]
    for g in range(groups):
        cols = slice(g * lanes, (g + 1) * lanes)
        t1, t2 = taps_ref[1, 0:1, cols], taps_ref[2, 0:1, cols]
        m2, m1 = past[8 + g : 9 + g], past[8 + groups + g : 9 + groups + g]
        added = jnp.where(row16 == 0, t1 * m1 + t2 * m2, jnp.where(row16 == 1, t2 * m1, 0.0))
        added = (masks_ref[len(pairs)] * added).astype(jnp.bfloat16)
        added_ref[g] = added
        cross_ref[g, cross_ref.shape[1] - EXTRA :, :] = added


def invert(place, core, inv_ref, zed, out_ref, conv):
    rows, lanes = conv.shape[0], out_ref.shape[2]
    table = inv_ref[pl.ds(pl.multiple_of((2 * place + core) * rows, rows), rows), :]
    conv[...] = jnp.dot(table, zed[...], preferred_element_type=jnp.float32).astype(jnp.bfloat16)
    for g in range(out_ref.shape[0]):
        out_ref[g, 0:rows, :] = conv[:, g * lanes : (g + 1) * lanes]


def invert_kernel(inv_ref, zed_ref, stay_ref, stay_later_ref, cross_later_ref, conv):
    cy, cc = lax.axis_index("cy"), lax.axis_index("cc")
    invert(cy, 1 - cc, inv_ref, zed_ref, cross_later_ref, conv)
    invert(1 - cy, cc, inv_ref, zed_ref, stay_ref, conv)
    invert(cy, cc, inv_ref, zed_ref, stay_later_ref, conv)


def pack_kernel(places, stay_ref, crossed_ref, *outs):
    lanes = stay_ref.shape[2]
    me = lax.axis_index("context")
    for offset, out_ref in zip(places, outs):
        rows = out_ref.shape[0]
        out_ref[:, 0:lanes] = stay_ref[me ^ offset, 0:rows, :]
        out_ref[:, lanes:] = crossed_ref[me ^ offset, 0:rows, :]


def project_kernel(places, own, columns, keep_ref, other_ref, added_ref, crossed_ref, w_ref, other_w_ref, *refs):
    backs, (out_ref, gated) = refs[:-2], refs[-2:]
    rows, lanes = backs[0].shape[0], backs[0].shape[1] // 2
    me, cy, cc = (lax.axis_index(axis) for axis in ("context", "cy", "cc"))
    first = ((cy if own else 1 - cy) == 0) & (cc == 0)
    row16 = lax.broadcasted_iota(jnp.int32, (EXTRA, 1), 0)
    for offset, back_ref in zip(places, backs):
        place = me ^ offset
        cols = lane_block(place, lanes)
        for at, (query_ref, edge_ref) in enumerate(((keep_ref, added_ref), (other_ref, crossed_ref))):
            query = query_ref[int(own), :, cols].astype(jnp.float32)
            conv = back_ref[:, at * lanes : (at + 1) * lanes].astype(jnp.float32)
            gated[at, :, cols] = (query * conv).astype(jnp.bfloat16)
            added = edge_ref[place, edge_ref.shape[1] - EXTRA :, :].astype(jnp.float32)
            top = query[0:EXTRA] + jnp.where(first, added, 0.0)
            gated[at, 0:EXTRA, cols] = (top * conv[0:EXTRA]).astype(jnp.bfloat16)
    total = jnp.dot(gated[0], w_ref[:, columns], preferred_element_type=jnp.float32)
    total = total + jnp.dot(gated[1], other_w_ref[:, columns], preferred_element_type=jnp.float32)
    out_ref[...] = total.astype(out_ref.dtype)


def sum_kernel(first, own_ref, got_ref, *refs):
    out_hbm, total, sems = refs[-3:]
    steps = sems.shape[0]
    rows, width = total.shape[0] // steps, total.shape[1]
    columns = slice(first, first + width)
    copies = []
    for i in range(steps):
        at = slice(i * rows, (i + 1) * rows)
        total[at, :] = (own_ref[at, columns] + got_ref[at, :].astype(jnp.float32)).astype(jnp.bfloat16)
        copies.append(pltpu.make_async_copy(total.at[at], out_hbm.at[at, columns], sems.at[i]))
        copies[-1].start()
    for copy in copies:
        copy.wait()


def swapped(x, axis, offset):
    return lax.ppermute(x, axis, [(i, i ^ offset) for i in range(lax.axis_size(axis))])


def in_hbm(x):
    return pltpu.with_memory_space_constraint(x, pltpu.HBM)


def turned(x, axis, by):
    peers = lax.axis_size(axis)
    return lax.ppermute(x, axis, [(i, (i + by) % peers) for i in range(peers)])


def spread(features, doc_start, short_taps, long_filter, w_out):
    groups = doc_start.shape[1]
    block_len = features.shape[1]
    channels = features.shape[3]
    dout = w_out.shape[1]
    lanes = channels // groups
    streams = jnp.transpose(features[0], (1, 0, 2))
    rows = block_len // PLACES
    fwd = jnp.asarray(spectrum_table(block_len))
    inv = jnp.asarray(outputs_table(block_len))
    lags = min(SEGS + 1, groups)
    piece_rows = block_len + edge_rows(groups)

    def like(*shape):
        return jax.ShapeDtypeStruct(shape, jnp.bfloat16)

    offsets = tuple(range(groups // 2, groups)) + tuple(range(groups // 2 - 1, -1, -1))
    far, near = offsets[: groups // 2], offsets[groups // 2 :]

    def products(places, *filters):
        return pl.pallas_call(
            functools.partial(product_kernel, groups, places),
            in_specs=[HBM] * (2 + len(filters)),
            out_specs=[VMEM] * (len(filters) + len(places)),
            out_shape=[like(lanes, x.shape[1]) for x in filters] + [like(piece_rows, lanes)] * len(places),
            scratch_shapes=[
                pltpu.VMEM((len(places), 2, block_len, lanes), jnp.bfloat16),
                pltpu.VMEM((EXTRA, channels), jnp.bfloat16),
                pltpu.VMEM(short_taps.shape, jnp.float32),
                pltpu.VMEM((block_len + 8, lanes), jnp.float32),
                pltpu.SemaphoreType.DMA((len(places), 2)),
                pltpu.SemaphoreType.DMA,
                pltpu.SemaphoreType.DMA,
                pltpu.SemaphoreType.DMA,
            ],
            compiler_params=PARAMS,
            name="product",
        )(in_hbm(streams), in_hbm(short_taps), *map(in_hbm, filters))

    own_taps, *sent = products(far, long_filter)
    sent += products(near)

    def exchanged(places, pieces):
        return [swapped(piece, "context", k) if k else piece for k, piece in zip(places, pieces)]

    ins = exchanged(offsets, sent)
    back_offsets = (groups // 2,) + tuple(range(1, groups // 2)) + tuple(range(groups // 2 + 1, groups)) + (0,)

    dp = lax.axis_size("dp")
    all_taps = [own_taps] + [turned(own_taps, "dp", k) for k in range(1, dp)]
    other_w = swapped(w_out, "cc", 1)
    keep, send = pl.pallas_call(
        query_kernel,
        in_specs=[HBM, VMEM],
        out_specs=[VMEM] * 2,
        out_shape=[jax.ShapeDtypeStruct((2, rows, channels), jnp.float32), like(2, rows, channels)],
        scratch_shapes=[
            pltpu.VMEM((block_len, channels), jnp.bfloat16),
            pltpu.VMEM((block_len + 8, channels), jnp.float32),
            pltpu.VMEM((block_len, channels), jnp.float32),
            pltpu.SemaphoreType.DMA,
        ],
        compiler_params=PARAMS,
        name="smoothed_query",
    )(in_hbm(streams), short_taps)
    send, all_taps = lax.optimization_barrier((send, all_taps))
    other = swapped(send, "cc", 1)
    marks = len(document_pairs(groups, lags)) + 1
    spectra, masks = pl.pallas_call(
        functools.partial(filter_kernel, groups),
        in_specs=[SMEM] + [VMEM] * (1 + dp),
        out_specs=[VMEM] * 2,
        out_shape=[
            jax.ShapeDtypeStruct((lags, 2 * block_len, lanes), jnp.float32),
            jax.ShapeDtypeStruct((marks, EXTRA, lanes), jnp.float32),
        ],
        scratch_shapes=[pltpu.VMEM((SEGS, 2 * block_len, lanes), jnp.float32)],
        compiler_params=PARAMS,
        name="filter_spectra",
    )(doc_start, fwd, *all_taps)

    spectra, masks, *rest = lax.optimization_barrier((spectra, masks, *ins[: len(far)]))
    ins[: len(far)] = rest
    gathered = pl.pallas_call(
        functools.partial(gather_kernel, far),
        in_specs=[VMEM] * len(far),
        out_specs=[VMEM] * 2,
        out_shape=[
            like(block_len, channels),
            jax.ShapeDtypeStruct((groups, edge_rows(groups), lanes), jnp.float32),
        ],
        compiler_params=PARAMS,
        name="gather",
    )(*ins[: len(far)])
    cross, added, zed, _ = pl.pallas_call(
        functools.partial(conv_kernel, offsets, len(near)),
        in_specs=[VMEM] * (7 + len(near)),
        out_specs=[VMEM] * 4,
        out_shape=[
            like(groups, rows + EXTRA, lanes),
            like(groups, EXTRA, lanes),
            like(2 * block_len, channels),
            like(block_len, channels),
        ],
        input_output_aliases={1: 3},
        scratch_shapes=[
            pltpu.VMEM((groups, edge_rows(groups), lanes), jnp.float32),
            pltpu.VMEM((2 * block_len, channels), jnp.float32),
            pltpu.VMEM((rows, channels), jnp.bfloat16),
        ],
        compiler_params=PARAMS,
        name="long_conv",
    )(masks, *gathered, fwd, inv, short_taps, spectra, *ins[len(far) :])
    crossed = swapped(cross, "cc", 1)
    stay, stay_later, cross_later = pl.pallas_call(
        invert_kernel,
        in_specs=[VMEM] * 2,
        out_specs=[VMEM] * 3,
        out_shape=[like(groups, rows, lanes)] * 3,
        scratch_shapes=[pltpu.VMEM((rows, channels), jnp.bfloat16)],
        compiler_params=PARAMS,
        name="long_conv_rest",
    )(inv, zed)

    def packed(stay, crossed):
        return pl.pallas_call(
            functools.partial(pack_kernel, back_offsets),
            in_specs=[VMEM] * 2,
            out_specs=[VMEM] * groups,
            out_shape=[like(rows, 2 * lanes)] * groups,
            compiler_params=PARAMS,
            name="pack",
        )(stay, crossed)

    first = packed(stay, crossed)
    second = packed(stay_later, swapped(cross_later, "cc", 1))
    keep, *second = lax.optimization_barrier((keep, *second))

    def projected(own, columns, backs, dtype):
        width = columns.stop - columns.start
        return pl.pallas_call(
            functools.partial(project_kernel, back_offsets, own, columns),
            in_specs=[VMEM] * (6 + groups),
            out_specs=VMEM,
            out_shape=jax.ShapeDtypeStruct((rows, width), dtype),
            scratch_shapes=[pltpu.VMEM((2, rows, channels), jnp.bfloat16)],
            compiler_params=PARAMS,
            name="gate_project",
        )(keep, other, added, crossed, w_out, other_w, *backs)

    backs = exchanged(back_offsets, first)
    width = dout // 2
    halves = [slice(at, at + width) for at in range(0, dout, width)]
    gots = [swapped(projected(False, columns, backs, jnp.bfloat16), "cy", 1) for columns in halves]
    own = projected(True, slice(0, dout), exchanged(back_offsets, second), jnp.float32)
    steps = 4
    total = ()
    for columns, got in zip(halves, gots):
        total = pl.pallas_call(
            functools.partial(sum_kernel, columns.start),
            in_specs=[VMEM] * 2 + [HBM] * len(total),
            out_specs=HBM,
            out_shape=like(rows, dout),
            scratch_shapes=[pltpu.VMEM((rows, width), jnp.bfloat16), pltpu.SemaphoreType.DMA((steps,))],
            input_output_aliases={2: 0} if total else {},
            compiler_params=PARAMS,
            name="sum",
        )(own, got, *total)
        total = (total,)
    return total[0][None]


def passed_along(x, axis, by):
    peers = lax.axis_size(axis)
    pairs = [(i, i + by) for i in range(peers) if 0 <= i + by < peers]
    return lax.ppermute(x, axis, pairs)


def forward_table(block_len):
    width = 2 * block_len
    rows = jnp.arange(width)[:, None]
    cols = jnp.arange(width)[None, :]
    freq = rows % block_len
    nyq_row = rows == block_len
    freq = jnp.where(nyq_row, block_len, freq)
    angle = (freq * cols % width).astype(jnp.float32) * (2.0 * math.pi / width)
    return jnp.where(rows <= block_len, jnp.cos(angle), -jnp.sin(angle))


def inverse_table(block_len):
    width = 2 * block_len
    outputs = (jnp.arange(block_len) + block_len)[:, None]
    cols = jnp.arange(width)[None, :]
    freq = cols % block_len
    angle = (freq * outputs % width).astype(jnp.float32) * (2.0 * math.pi / width)
    nyq_sign = jnp.cos((block_len * outputs % width).astype(jnp.float32) * (2.0 * math.pi / width))
    real_part = jnp.where(cols == 0, 1.0, 2.0 * jnp.cos(angle))
    imag_part = jnp.where(cols == block_len, nyq_sign, -2.0 * jnp.sin(angle))
    return jnp.where(cols < block_len, real_part, imag_part) / width


def split_table(table):
    upper = table.astype(jnp.bfloat16)
    lower = (table - upper.astype(jnp.float32)).astype(jnp.bfloat16)
    return (upper, lower)


def in_place(features, doc_start, short_taps, long_filter, w_out):
    block_len = features.shape[1]
    channels = features.shape[3]
    group = lax.axis_index("context")
    position = jnp.arange(doc_start.shape[1])
    begins = jnp.where(position == 0, 1, doc_start[0])
    documents = jnp.cumsum(begins)

    def lookup(vector, where_at):
        return jnp.sum(jnp.where(position == where_at, vector, 0))

    own_doc = lookup(documents, group)
    own_begin = lookup(begins, group) == 1
    tails = passed_along(features[:, block_len - 2 :], "context", 1)
    tails = jnp.where(own_begin, jnp.zeros_like(tails), tails)
    extended = jnp.concatenate([tails, features], 1)[0].astype(jnp.float32)
    smoothed = (
        short_taps[0] * extended[2:]
        + short_taps[1] * extended[1:-1]
        + short_taps[2] * extended[:-2]
    )
    product = (smoothed[:, 1] * smoothed[:, 2]).astype(jnp.bfloat16)
    previous = passed_along(product, "context", 1)
    forward = forward_table(block_len)
    fwd_upper, fwd_lower = split_table(forward)
    earlier = previous
    earlier = jnp.where(own_begin, jnp.zeros_like(earlier), earlier)
    window = jnp.concatenate([earlier, product], 0)
    own_spectrum = jnp.dot(fwd_upper, window, preferred_element_type=jnp.float32) + jnp.dot(
        fwd_lower, window, preferred_element_type=jnp.float32
    )
    sources = [own_spectrum]
    for offset in range(1, SEGS):
        sources.append(
            passed_along(own_spectrum.astype(jnp.bfloat16), "context", offset).astype(
                own_spectrum.dtype
            )
        )
    tap_upper = fwd_upper[:, :block_len]
    tap_lower = fwd_lower[:, :block_len]
    all_taps = lax.all_gather(long_filter, "dp", axis=1, tiled=True).reshape(
        channels, -1, block_len
    )
    filt_spectra = jnp.einsum(
        "fm,ckm->kfc", tap_upper, all_taps, preferred_element_type=jnp.float32
    ) + jnp.einsum("fm,ckm->kfc", tap_lower, all_taps, preferred_element_type=jnp.float32)
    dc_row = (jnp.arange(block_len) == 0)[:, None]
    total_real = jnp.zeros((block_len, channels), jnp.float32)
    total_imag = jnp.zeros((block_len, channels), jnp.float32)
    for offset in range(SEGS):
        source_group = group - offset
        keeping = (source_group >= 0) & (lookup(documents, source_group) == own_doc)
        filt_real = filt_spectra[offset, :block_len]
        filt_imag = filt_spectra[offset, block_len:]
        src_real = sources[offset][:block_len]
        src_imag = sources[offset][block_len:]
        crossed = filt_imag * src_imag
        part_real = filt_real * src_real - jnp.where(dc_row, 0.0, crossed)
        part_imag = jnp.where(dc_row, crossed, filt_real * src_imag + filt_imag * src_real)
        total_real = total_real + jnp.where(keeping, part_real, 0.0)
        total_imag = total_imag + jnp.where(keeping, part_imag, 0.0)
    conv = jnp.dot(
        inverse_table(block_len),
        jnp.concatenate([total_real, total_imag], 0),
        precision=lax.Precision.HIGH,
    )
    gated = (smoothed[:, 0] * conv).astype(jnp.bfloat16)
    partial_out = jnp.dot(gated, w_out, preferred_element_type=jnp.float32)
    summed = lax.psum_scatter(
        lax.optimization_barrier(partial_out.astype(jnp.bfloat16))
        .astype(jnp.float32)
        .astype(jnp.bfloat16),
        "channel",
        scatter_dimension=0,
        tiled=True,
    )
    return summed[None]


def power_of_two(n):
    return n > 1 and n & (n - 1) == 0


def solution(mesh):
    sizes = dict(mesh.shape)

    def run(features, doc_start, short_taps, long_filter, w_out):
        groups, peers = sizes["context"], sizes["channel"]
        channels = features.shape[3] // peers
        if (
            power_of_two(groups)
            and peers == PLACES
            and doc_start.shape[1] == groups
            and channels % (LANES * groups) == 0
            and SEGS % sizes["dp"] == 0
        ):
            assert mesh.axis_names == ("context", "channel", "dp")
            split = Mesh(mesh.devices.reshape(groups, 2, 2, -1), ("context", "cy", "cc", "dp"))
            body, over, channel = spread, split, ("cy", "cc")
        else:
            body, over, channel = in_place, mesh, ("channel",)
        return jax.shard_map(
            body,
            mesh=over,
            in_specs=(
                P("dp", "context", None, channel),
                P("dp", None),
                P(None, None, channel),
                P(channel, "dp"),
                P(channel, None),
            ),
            out_specs=P("dp", ("context",) + channel, None),
            check_vma=False,
        )(features, doc_start, short_taps, long_filter, w_out)

    return run
```

profile of v0, /device:TPU:0, one launch (start us, length us, event | category | flops | bytes accessed | tf_op | source)
XLA Modules:
  0.0 46.9 jit_solution(11565539387202168630)
XLA Ops:
  0.5 1.4 %product.2 = (bf16[128,1024]{1,0:T(8,128)(2,1)S(1)}, bf16[528,128]{1,0:T(8,128)(2,1)S(1)}, bf16[528,128]{1,0:T(8,128)(2,1)S(1)}) custom-call(bf16[3,512,512]{2,1,0:T(8,128)(2,1)} %bitcast.4, f32[3,3,512]{2,1,0:T(4,128)} %taps_ref.3, bf16[512,1024]{1,0:T(8,128)(2,1)} %refs_0_.1), custom_call_target="tpu_custom_call" | custom-call | tf_op jit(solution)/shard_map/product/pallas_call | solution.py:328
  1.9 2.6 %collective-permute-start = (bf16[128,1024]{1,0:T(8,128)(2,1)S(1)}, bf16[128,1024]{1,0:T(8,128)(2,1)S(1)}, u32[]{:S(2)}, u32[]{:S(2)}) collective-permute-start(bf16[128,1024]{1,0:T(8,128)(2,1)S(1)} %get-tuple-element.45.refs_0_), channel_id=1, source_target_pairs={{0,1},{1,0},{2,3},{3,2},{4,5},{5,4},{6,7},{7,6},{8,9},{9,8},{10,11... | collective-permute-start | bytes 786440 | tf_op jit(solution)/shard_map/ppermute | solution.py:305
  4.5 2.6 %collective-permute-start.1 = (bf16[528,128]{1,0:T(8,128)(2,1)S(1)}, bf16[528,128]{1,0:T(8,128)(2,1)S(1)}, u32[]{:S(2)}, u32[]{:S(2)}) collective-permute-start(bf16[528,128]{1,0:T(8,128)(2,1)S(1)} %get-tuple-element.49), channel_id=1, source_target_pairs={{0,16},{8,24},{16,0},{24,8},{1,17},{9,25},{17,1},{25,9},{2,18},{10... | collective-permute-start | bytes 405512 | tf_op jit(solution)/shard_map/ppermute | solution.py:296
  7.1 1.4 %collective-permute-start.2 = (bf16[528,128]{1,0:T(8,128)(2,1)S(1)}, bf16[528,128]{1,0:T(8,128)(2,1)S(1)}, u32[]{:S(2)}, u32[]{:S(2)}) collective-permute-start(bf16[528,128]{1,0:T(8,128)(2,1)S(1)} %get-tuple-element.50), channel_id=1, source_target_pairs={{0,24},{8,16},{16,8},{24,0},{1,25},{9,17},{17,9},{25,1},{2,26},{10... | collective-permute-start | bytes 405512 | tf_op jit(solution)/shard_map/ppermute | solution.py:296
  8.4 1.4 %product.3 = (bf16[528,128]{1,0:T(8,128)(2,1)S(1)}, bf16[528,128]{1,0:T(8,128)(2,1)S(1)}) custom-call(bf16[3,512,512]{2,1,0:T(8,128)(2,1)} %bitcast.5, f32[3,3,512]{2,1,0:T(4,128)} %taps_ref.3), custom_call_target="tpu_custom_call" | custom-call | tf_op jit(solution)/shard_map/product/pallas_call | solution.py:328
  10.1 1.8 %smoothed_query.1 = (f32[2,128,512]{2,1,0:T(8,128)S(1)}, bf16[2,128,512]{2,1,0:T(8,128)(2,1)S(1)}) custom-call(bf16[3,512,512]{2,1,0:T(8,128)(2,1)} %bitcast.6, f32[3,3,512]{2,1,0:T(4,128)S(1)} %copy-done.3), custom_call_target="tpu_custom_call" | custom-call | tf_op jit(solution)/shard_map/smoothed_query/pallas_call | solution.py:359
  12.0 2.4 %filter_spectra.1 = (f32[4,1024,128]{2,1,0:T(8,128)S(1)}, f32[7,16,128]{2,1,0:T(8,128)S(1)}) custom-call(s32[1,4]{1,0:T(1,128)S(1)} %copy-done.4, bf16[1024,512]{1,0:T(8,128)(2,1)S(1)} %copy-done.2, bf16[128,1024]{1,0:T(8,128)(2,1)S(1)} %get-tuple-element.45.refs_0_, bf16[128,1024]{1,0:T(8,128)(2,1)S(1)} %collective-permute-done.refs_1_), custom_call_target="tpu_custom_call" | custom-call | tf_op jit(solution)/shard_map/filter_spectra/pallas_call | solution.py:376
  14.4 3.2 %collective-permute-done.1.refs_0_ = bf16[528,128]{1,0:T(8,128)(2,1)S(1)} collective-permute-done((bf16[528,128]{1,0:T(8,128)(2,1)S(1)}, bf16[528,128]{1,0:T(8,128)(2,1)S(1)}, u32[]{:S(2)}, u32[]{:S(2)}) %collective-permute-start.1) | collective-permute-done | bytes 135200 | tf_op jit(solution)/shard_map/ppermute | solution.py:296
  17.7 1.7 %collective-permute-done.3.refs_0_ = bf16[528,128]{1,0:T(8,128)(2,1)S(1)} collective-permute-done((bf16[528,128]{1,0:T(8,128)(2,1)S(1)}, bf16[528,128]{1,0:T(8,128)(2,1)S(1)}, u32[]{:S(2)}, u32[]{:S(2)}) %collective-permute-start.3) | collective-permute-done | bytes 135200 | tf_op jit(solution)/shard_map/ppermute | solution.py:296
  19.4 1.8 %long_conv.1 = (bf16[4,144,128]{2,1,0:T(8,128)(2,1)S(1)}, bf16[4,16,128]{2,1,0:T(8,128)(2,1)S(1)}, bf16[1024,512]{1,0:T(8,128)(2,1)S(1)}, bf16[512,512]{1,0:T(8,128)(2,1)S(1)}) custom-call(f32[7,16,128]{2,1,0:T(8,128)S(1)} %get-tuple-element.51.masks_ref, bf16[512,512]{1,0:T(8,128)(2,1)S(1)} %get-tuple-element.54.far_ref, ...), custom_call_target="tpu_custom_call", output_to_operand_aliasing={{3}: (1, {})} | custom-call | tf_op jit(solution)/shard_map/long_conv/pallas_call | solution.py:402
  21.3 0.7 %long_conv_rest.1 = (bf16[4,128,128]{2,1,0:T(8,128)(2,1)S(1)}, bf16[4,128,128]{2,1,0:T(8,128)(2,1)S(1)}, bf16[4,128,128]{2,1,0:T(8,128)(2,1)S(1)}) custom-call(bf16[512,1024]{1,0:T(8,128)(2,1)S(1)} %copy-done.1, bf16[1024,512]{1,0:T(8,128)(2,1)S(1)} %get-tuple-element.59.zed_ref), custom_call_target="tpu_custom_call" | custom-call | tf_op jit(solution)/shard_map/long_conv_rest/pallas_call | solution.py:422
  22.7 3.1 %collective-permute-start.11 = (bf16[128,256]{1,0:T(8,128)(2,1)S(1)}, bf16[128,256]{1,0:T(8,128)(2,1)S(1)}, u32[]{:S(2)}, u32[]{:S(2)}) collective-permute-start(bf16[128,256]{1,0:T(8,128)(2,1)S(1)} %get-tuple-element.75), channel_id=1, source_target_pairs={{0,16},{8,24},{16,0},{24,8},{1,17},{9,25},{17,1},{25,9},{2,18},{10... | collective-permute-start | bytes 196616 | tf_op jit(solution)/shard_map/ppermute | solution.py:296
  25.9 1.0 %collective-permute-start.12 = (bf16[128,256]{1,0:T(8,128)(2,1)S(1)}, bf16[128,256]{1,0:T(8,128)(2,1)S(1)}, u32[]{:S(2)}, u32[]{:S(2)}) collective-permute-start(bf16[128,256]{1,0:T(8,128)(2,1)S(1)} %get-tuple-element.76), channel_id=1, source_target_pairs={{0,8},{8,0},{16,24},{24,16},{1,9},{9,1},{17,25},{25,17},{2,10},{10... | collective-permute-start | bytes 196616 | tf_op jit(solution)/shard_map/ppermute | solution.py:296
  27.5 2.3 %collective-permute-done.11.refs_0_ = bf16[128,256]{1,0:T(8,128)(2,1)S(1)} collective-permute-done((bf16[128,256]{1,0:T(8,128)(2,1)S(1)}, bf16[128,256]{1,0:T(8,128)(2,1)S(1)}, u32[]{:S(2)}, u32[]{:S(2)}) %collective-permute-start.11) | collective-permute-done | bytes 65568 | tf_op jit(solution)/shard_map/ppermute | solution.py:296
  29.8 0.8 %collective-permute-done.12.refs_1_ = bf16[128,256]{1,0:T(8,128)(2,1)S(1)} collective-permute-done((bf16[128,256]{1,0:T(8,128)(2,1)S(1)}, bf16[128,256]{1,0:T(8,128)(2,1)S(1)}, u32[]{:S(2)}, u32[]{:S(2)}) %collective-permute-start.12) | collective-permute-done | bytes 65568 | tf_op jit(solution)/shard_map/ppermute | solution.py:296
  30.6 2.3 %collective-permute-done.13.refs_2_ = bf16[128,256]{1,0:T(8,128)(2,1)S(1)} collective-permute-done((bf16[128,256]{1,0:T(8,128)(2,1)S(1)}, bf16[128,256]{1,0:T(8,128)(2,1)S(1)}, u32[]{:S(2)}, u32[]{:S(2)}) %collective-permute-start.13) | collective-permute-done | bytes 65568 | tf_op jit(solution)/shard_map/ppermute | solution.py:296
  33.5 1.6 %collective-permute-start.15 = (bf16[128,1024]{1,0:T(8,128)(2,1)S(1)}, bf16[128,1024]{1,0:T(8,128)(2,1)S(1)}, u32[]{:S(2)}, u32[]{:S(2)}) collective-permute-start(bf16[128,1024]{1,0:T(8,128)(2,1)S(1)} %gate_project.5), channel_id=1, source_target_pairs={{0,4},{4,0},{1,5},{5,1},{2,6},{6,2},{3,7},{7,3},{8,12},{12,8},{9,1... | collective-permute-start | bytes 786440 | tf_op jit(solution)/shard_map/ppermute | solution.py:296
  36.2 1.7 %collective-permute-start.8 = (bf16[128,256]{1,0:T(8,128)(2,1)S(1)}, bf16[128,256]{1,0:T(8,128)(2,1)S(1)}, u32[]{:S(2)}, u32[]{:S(2)}) collective-permute-start(bf16[128,256]{1,0:T(8,128)(2,1)S(1)} %get-tuple-element.70), channel_id=1, source_target_pairs={{0,16},{8,24},{16,0},{24,8},{1,17},{9,25},{17,1},{25,9},{2,18},{10... | collective-permute-start | bytes 196616 | tf_op jit(solution)/shard_map/ppermute | solution.py:296
  38.5 2.1 %collective-permute-start.10 = (bf16[128,256]{1,0:T(8,128)(2,1)S(1)}, bf16[128,256]{1,0:T(8,128)(2,1)S(1)}, u32[]{:S(2)}, u32[]{:S(2)}) collective-permute-start(bf16[128,256]{1,0:T(8,128)(2,1)S(1)} %get-tuple-element.72), channel_id=1, source_target_pairs={{0,24},{8,16},{16,8},{24,0},{1,25},{9,17},{17,9},{25,1},{2,26},{10... | collective-permute-start | bytes 196616 | tf_op jit(solution)/shard_map/ppermute | solution.py:296
  40.5 2.2 %collective-permute-done.8.refs_0_ = bf16[128,256]{1,0:T(8,128)(2,1)S(1)} collective-permute-done((bf16[128,256]{1,0:T(8,128)(2,1)S(1)}, bf16[128,256]{1,0:T(8,128)(2,1)S(1)}, u32[]{:S(2)}, u32[]{:S(2)}) %collective-permute-start.8) | collective-permute-done | bytes 65568 | tf_op jit(solution)/shard_map/ppermute | solution.py:296
  42.9 1.6 %collective-permute-done.10.refs_2_ = bf16[128,256]{1,0:T(8,128)(2,1)S(1)} collective-permute-done((bf16[128,256]{1,0:T(8,128)(2,1)S(1)}, bf16[128,256]{1,0:T(8,128)(2,1)S(1)}, u32[]{:S(2)}, u32[]{:S(2)}) %collective-permute-start.10) | collective-permute-done | bytes 65568 | tf_op jit(solution)/shard_map/ppermute | solution.py:296
  44.6 0.8 %gate_project.3.own_ref = f32[128,2048]{1,0:T(8,128)S(1)} custom-call(f32[2,128,512]{2,1,0:T(8,128)S(1)} %get-tuple-element.66.keep_ref, bf16[2,128,512]{2,1,0:T(8,128)(2,1)S(1)} %collective-permute-done.5.other_ref, bf16[4,16,128]{2,1,0:T(8,128)(2,1)S(1)} %get-tuple-element.68.added_ref, bf16[4,144,128]{2,1,0:T(8,128)(2,1)S(1)} %collective-permute-done.6.crossed_ref, ...), custom_call_target="tpu_custom_call" | custom-call | tf_op jit(solution)/shard_map/gate_project/pallas_call | solution.py:448
  45.4 0.7 %sum.2.refs_0_ = bf16[128,2048]{1,0:T(8,128)(2,1)} custom-call(f32[128,2048]{1,0:T(8,128)S(1)} %gate_project.3.own_ref, bf16[128,1024]{1,0:T(8,128)(2,1)S(1)} %collective-permute-done.15.got_ref), custom_call_target="tpu_custom_call" | custom-call | tf_op jit(solution)/shard_map/sum/pallas_call | solution.py:466
  46.1 0.7 %sum.3 = bf16[128,2048]{1,0:T(8,128)(2,1)} custom-call(f32[128,2048]{1,0:T(8,128)S(1)} %gate_project.3.own_ref, bf16[128,1024]{1,0:T(8,128)(2,1)S(1)} %collective-permute-done.14.got_ref, bf16[128,2048]{1,0:T(8,128)(2,1)} %sum.2.refs_0_), custom_call_target="tpu_custom_call", output_to_operand_aliasing={{}: (2, {})} | custom-call | tf_op jit(solution)/shard_map/sum/pallas_call | solution.py:466
  (32 shorter events, 4.8 us)
Async XLA Ops:
  0.0 32.9 %collective-permute-start.7 = (bf16[512,2048]{1,0:T(8,128)(2,1)}, bf16[512,2048]{1,0:T(8,128)(2,1)S(1)}, u32[]{:S(2)}, u32[]{:S(2)}) collective-permute-start(bf16[512,2048]{1,0:T(8,128)(2,1)} %w_ref.5), channel_id=1, source_target_pairs={{0,2},{2,0},{1,3},{3,1},{4,6},{6,4},{5,7},{7,5},{8,10},{10,8},{9,1... | collective-permute-start | bytes 6291464 | tf_op jit(solution)/shard_map/ppermute | solution.py:296
  0.5 9.7 %copy-start.3 = (f32[3,3,512]{2,1,0:T(4,128)S(1)}, f32[3,3,512]{2,1,0:T(4,128)}, u32[]{:S(2)}) copy-start(f32[3,3,512]{2,1,0:T(4,128)} %taps_ref.3) | copy-start | bytes 55300
  1.9 10.1 %copy-start.2 = (bf16[1024,512]{1,0:T(8,128)(2,1)S(1)}, bf16[1024,512]{1,0:T(8,128)(2,1)}, u32[]{:S(2)}) copy-start(bf16[1024,512]{1,0:T(8,128)(2,1)} %constant.4.clone.fwd_ref) | copy-start | bytes 3145732
  1.9 10.1 %copy-start.4 = (s32[1,4]{1,0:T(1,128)S(1)}, s32[1,4]{1,0:T(1,128)}, u32[]{:S(2)}) copy-start(s32[1,4]{1,0:T(1,128)} %begin_ref.1) | copy-start | bytes 52
  1.9 10.0 %collective-permute-start = (bf16[128,1024]{1,0:T(8,128)(2,1)S(1)}, bf16[128,1024]{1,0:T(8,128)(2,1)S(1)}, u32[]{:S(2)}, u32[]{:S(2)}) collective-permute-start(bf16[128,1024]{1,0:T(8,128)(2,1)S(1)} %get-tuple-element.45.refs_0_), channel_id=1, source_target_pairs={{0,1},{1,0},{2,3},{3,2},{4,5},{5,4},{6,7},{7,6},{8,9},{9,8},{10,11... | collective-permute-start | bytes 786440 | tf_op jit(solution)/shard_map/ppermute | solution.py:305
  4.5 13.2 %collective-permute-start.1 = (bf16[528,128]{1,0:T(8,128)(2,1)S(1)}, bf16[528,128]{1,0:T(8,128)(2,1)S(1)}, u32[]{:S(2)}, u32[]{:S(2)}) collective-permute-start(bf16[528,128]{1,0:T(8,128)(2,1)S(1)} %get-tuple-element.49), channel_id=1, source_target_pairs={{0,16},{8,24},{16,0},{24,8},{1,17},{9,25},{17,1},{25,9},{2,18},{10... | collective-permute-start | bytes 405512 | tf_op jit(solution)/shard_map/ppermute | solution.py:296
  7.1 10.6 %collective-permute-start.2 = (bf16[528,128]{1,0:T(8,128)(2,1)S(1)}, bf16[528,128]{1,0:T(8,128)(2,1)S(1)}, u32[]{:S(2)}, u32[]{:S(2)}) collective-permute-start(bf16[528,128]{1,0:T(8,128)(2,1)S(1)} %get-tuple-element.50), channel_id=1, source_target_pairs={{0,24},{8,16},{16,8},{24,0},{1,25},{9,17},{17,9},{25,1},{2,26},{10... | collective-permute-start | bytes 405512 | tf_op jit(solution)/shard_map/ppermute | solution.py:296
  9.8 9.6 %copy-start.1 = (bf16[512,1024]{1,0:T(8,128)(2,1)S(1)}, bf16[512,1024]{1,0:T(8,128)(2,1)}, u32[]{:S(2)}) copy-start(bf16[512,1024]{1,0:T(8,128)(2,1)} %constant.5.clone.inv_ref) | copy-start | bytes 3145732
  9.8 9.6 %collective-permute-start.3 = (bf16[528,128]{1,0:T(8,128)(2,1)S(1)}, bf16[528,128]{1,0:T(8,128)(2,1)S(1)}, u32[]{:S(2)}, u32[]{:S(2)}) collective-permute-start(bf16[528,128]{1,0:T(8,128)(2,1)S(1)} %get-tuple-element.57), channel_id=1, source_target_pairs={{0,8},{8,0},{16,24},{24,16},{1,9},{9,1},{17,25},{25,17},{2,10},{10... | collective-permute-start | bytes 405512 | tf_op jit(solution)/shard_map/ppermute | solution.py:296
  11.9 21.0 %collective-permute-start.5 = (bf16[2,128,512]{2,1,0:T(8,128)(2,1)S(1)}, bf16[2,128,512]{2,1,0:T(8,128)(2,1)S(1)}, u32[]{:S(2)}, u32[]{:S(2)}) collective-permute-start(bf16[2,128,512]{2,1,0:T(8,128)(2,1)S(1)} %get-tuple-element.67), channel_id=1, source_target_pairs={{0,2},{2,0},{1,3},{3,1},{4,6},{6,4},{5,7},{7,5},{8,10},{10,8},{9,1... | collective-permute-start | bytes 786440 | tf_op jit(solution)/shard_map/ppermute | solution.py:296
  21.2 11.7 %copy-start = (bf16[512,2048]{1,0:T(8,128)(2,1)S(1)}, bf16[512,2048]{1,0:T(8,128)(2,1)}, u32[]{:S(2)}) copy-start(bf16[512,2048]{1,0:T(8,128)(2,1)} %w_ref.5) | copy-start | bytes 6291460
  21.2 1.4 %collective-permute-start.6 = (bf16[4,144,128]{2,1,0:T(8,128)(2,1)S(1)}, bf16[4,144,128]{2,1,0:T(8,128)(2,1)S(1)}, u32[]{:S(2)}, u32[]{:S(2)}) collective-permute-start(bf16[4,144,128]{2,1,0:T(8,128)(2,1)S(1)} %get-tuple-element.69), channel_id=1, source_target_pairs={{0,2},{2,0},{1,3},{3,1},{4,6},{6,4},{5,7},{7,5},{8,10},{10,8},{9,1... | collective-permute-start | bytes 442376 | tf_op jit(solution)/shard_map/ppermute | solution.py:296
  22.0 4.9 %collective-permute-start.4 = (bf16[4,128,128]{2,1,0:T(8,128)(2,1)S(1)}, bf16[4,128,128]{2,1,0:T(8,128)(2,1)S(1)}, u32[]{:S(2)}, u32[]{:S(2)}) collective-permute-start(bf16[4,128,128]{2,1,0:T(8,128)(2,1)S(1)} %get-tuple-element.61), channel_id=1, source_target_pairs={{0,2},{2,0},{1,3},{3,1},{4,6},{6,4},{5,7},{7,5},{8,10},{10,8},{9,1... | collective-permute-start | bytes 393224 | tf_op jit(solution)/shard_map/ppermute | solution.py:296
  22.7 7.1 %collective-permute-start.11 = (bf16[128,256]{1,0:T(8,128)(2,1)S(1)}, bf16[128,256]{1,0:T(8,128)(2,1)S(1)}, u32[]{:S(2)}, u32[]{:S(2)}) collective-permute-start(bf16[128,256]{1,0:T(8,128)(2,1)S(1)} %get-tuple-element.75), channel_id=1, source_target_pairs={{0,16},{8,24},{16,0},{24,8},{1,17},{9,25},{17,1},{25,9},{2,18},{10... | collective-permute-start | bytes 196616 | tf_op jit(solution)/shard_map/ppermute | solution.py:296
  25.9 4.8 %collective-permute-start.12 = (bf16[128,256]{1,0:T(8,128)(2,1)S(1)}, bf16[128,256]{1,0:T(8,128)(2,1)S(1)}, u32[]{:S(2)}, u32[]{:S(2)}) collective-permute-start(bf16[128,256]{1,0:T(8,128)(2,1)S(1)} %get-tuple-element.76), channel_id=1, source_target_pairs={{0,8},{8,0},{16,24},{24,16},{1,9},{9,1},{17,25},{25,17},{2,10},{10... | collective-permute-start | bytes 196616 | tf_op jit(solution)/shard_map/ppermute | solution.py:296
  26.8 6.1 %collective-permute-start.13 = (bf16[128,256]{1,0:T(8,128)(2,1)S(1)}, bf16[128,256]{1,0:T(8,128)(2,1)S(1)}, u32[]{:S(2)}, u32[]{:S(2)}) collective-permute-start(bf16[128,256]{1,0:T(8,128)(2,1)S(1)} %get-tuple-element.77), channel_id=1, source_target_pairs={{0,24},{8,16},{16,8},{24,0},{1,25},{9,17},{17,9},{25,1},{2,26},{10... | collective-permute-start | bytes 196616 | tf_op jit(solution)/shard_map/ppermute | solution.py:296
  33.5 11.9 %collective-permute-start.15 = (bf16[128,1024]{1,0:T(8,128)(2,1)S(1)}, bf16[128,1024]{1,0:T(8,128)(2,1)S(1)}, u32[]{:S(2)}, u32[]{:S(2)}) collective-permute-start(bf16[128,1024]{1,0:T(8,128)(2,1)S(1)} %gate_project.5), channel_id=1, source_target_pairs={{0,4},{4,0},{1,5},{5,1},{2,6},{6,2},{3,7},{7,3},{8,12},{12,8},{9,1... | collective-permute-start | bytes 786440 | tf_op jit(solution)/shard_map/ppermute | solution.py:296
  35.6 10.5 %collective-permute-start.14 = (bf16[128,1024]{1,0:T(8,128)(2,1)S(1)}, bf16[128,1024]{1,0:T(8,128)(2,1)S(1)}, u32[]{:S(2)}, u32[]{:S(2)}) collective-permute-start(bf16[128,1024]{1,0:T(8,128)(2,1)S(1)} %gate_project.4), channel_id=1, source_target_pairs={{0,4},{4,0},{1,5},{5,1},{2,6},{6,2},{3,7},{7,3},{8,12},{12,8},{9,1... | collective-permute-start | bytes 786440 | tf_op jit(solution)/shard_map/ppermute | solution.py:296
  36.2 6.6 %collective-permute-start.8 = (bf16[128,256]{1,0:T(8,128)(2,1)S(1)}, bf16[128,256]{1,0:T(8,128)(2,1)S(1)}, u32[]{:S(2)}, u32[]{:S(2)}) collective-permute-start(bf16[128,256]{1,0:T(8,128)(2,1)S(1)} %get-tuple-element.70), channel_id=1, source_target_pairs={{0,16},{8,24},{16,0},{24,8},{1,17},{9,25},{17,1},{25,9},{2,18},{10... | collective-permute-start | bytes 196616 | tf_op jit(solution)/shard_map/ppermute | solution.py:296
  37.9 5.1 %collective-permute-start.9 = (bf16[128,256]{1,0:T(8,128)(2,1)S(1)}, bf16[128,256]{1,0:T(8,128)(2,1)S(1)}, u32[]{:S(2)}, u32[]{:S(2)}) collective-permute-start(bf16[128,256]{1,0:T(8,128)(2,1)S(1)} %get-tuple-element.71), channel_id=1, source_target_pairs={{0,8},{8,0},{16,24},{24,16},{1,9},{9,1},{17,25},{25,17},{2,10},{10... | collective-permute-start | bytes 196616 | tf_op jit(solution)/shard_map/ppermute | solution.py:296
  38.5 6.1 %collective-permute-start.10 = (bf16[128,256]{1,0:T(8,128)(2,1)S(1)}, bf16[128,256]{1,0:T(8,128)(2,1)S(1)}, u32[]{:S(2)}, u32[]{:S(2)}) collective-permute-start(bf16[128,256]{1,0:T(8,128)(2,1)S(1)} %get-tuple-element.72), channel_id=1, source_target_pairs={{0,24},{8,16},{16,8},{24,0},{1,25},{9,17},{17,9},{25,1},{2,26},{10... | collective-permute-start | bytes 196616 | tf_op jit(solution)/shard_map/ppermute | solution.py:296
where the time goes:
time: 47 us; the launch traced here: 46.9 us
  starting transfers between devices  19.2 us (41%)
  waiting for transfers between devices  14.6 us (31%)
  Pallas kernels  12.9 us (27%)
    ppermute x15, starting transfers between devices, swapped(): lax.ppermute(x, axis, [(i, i ^ offset) for i in range(lax.axis_size(axis))])  16.6 us
    ppermute x15, waiting for transfers between devices, swapped(): lax.ppermute(x, axis, [(i, i ^ offset) for i in range(lax.axis_size(axis))])  14.6 us
    pallas_call x2, Pallas kernels, products(): pl.pallas_call(functools.partial(product_kernel, groups, places), in_spec...  2.83 us
    ppermute x1, starting transfers between devices, turned(): return lax.ppermute(x, axis, [(i, (i + by) % peers) for i in range(peers)])  2.55 us
    pallas_call x1, Pallas kernels, spread(): pl.pallas_call(functools.partial(filter_kernel, groups), in_specs=[SMEM]...  2.37 us
    pallas_call x3, Pallas kernels, projected(): pl.pallas_call(functools.partial(project_kernel, back_offsets, own, colum...  1.84 us
    pallas_call x1, Pallas kernels, spread(): pl.pallas_call(functools.partial(conv_kernel, offsets, len(near)), in_spe...  1.81 us
    pallas_call x1, Pallas kernels, spread(): pl.pallas_call(query_kernel, in_specs=[HBM, VMEM], out_specs=[VMEM] * 2,...  1.78 us
  transfers between devices with their start and end apart: 16, of which 9 were waited for; matrix products, arithmetic and copies ran while one was open for 0% of the time, Pallas kernels for 25%

commit v1 on v0

--- a/solution.py
+++ b/solution.py
@@ -62,31 +62,46 @@
 
     taps_copy = started(taps_hbm, taps_ref, taps_sem)
     q_copy = started(streams_hbm.at[0, n - EXTRA : n], q, q_sem)
+    half = n // 2
     loads = [
         [
-            started(streams_hbm.at[s + 1, :, lane_block(me ^ offset, lanes)], kv.at[i, s], sems.at[i, s])
-            for s in range(2)
+            [
+                started(
+                    streams_hbm.at[s + 1, h * half : (h + 1) * half, lane_block(me ^ offset, lanes)],
+                    kv.at[i, s, h * half : (h + 1) * half],
+                    sems.at[i, s, h],
+                )
+                for s in range(2)
+            ]
+            for h in range(2)
         ]
         for i, offset in enumerate(offsets)
     ]
     if filter_refs:
         filter_copy = started(filter_refs[0].at[lane_block(me, lanes)], filter_refs[1], filter_sem)
+    ext[:, 0:8, :] = jnp.zeros((2, 8, lanes), jnp.float32)
     taps_copy.wait()
-    q_copy.wait()
-    last = q[...].astype(jnp.float32)[EXTRA - 2 :]
-    tails = [last[t : t + 1, g * lanes : (g + 1) * lanes] for t in range(2) for g in range(groups)]
     for i, offset in enumerate(offsets):
         taps = taps_ref[:, :, lane_block(me ^ offset, lanes)]
-        smoothed, edges = [], []
+        for h in range(2):
+            at = h * half
+            smoothed = []
+            for s in range(2):
+                loads[i][h][s].wait()
+                x = kv[i, s, at : at + half].astype(jnp.float32)
+                t = [taps[j, s + 1 : s + 2] for j in range(3)]
+                ext[s, 8 + at : 8 + at + half, :] = x
+                smoothed.append(
+                    t[0] * x + t[1] * ext[s, 7 + at : 7 + at + half, :] + t[2] * ext[s, 6 + at : 6 + at + half, :]
+                )
+            outs[i][at : at + half, :] = (smoothed[0] * smoothed[1]).astype(jnp.bfloat16)
+        if i == 0:
+            q_copy.wait()
+            last = q[...].astype(jnp.float32)[EXTRA - 2 :]
+            tails = [last[t : t + 1, g * lanes : (g + 1) * lanes] for t in range(2) for g in range(groups)]
+        edges = []
         for s in range(2):
-            loads[i][s].wait()
-            x = kv[i, s].astype(jnp.float32)
-            t = [taps[j, s + 1 : s + 2] for j in range(3)]
-            ext[8:, :] = x
-            ext[0:8, :] = jnp.zeros((8, lanes), jnp.float32)
-            smoothed.append(t[0] * x + t[1] * ext[7 : 7 + n, :] + t[2] * ext[6 : 6 + n, :])
-            edges += [x[0:2], x[n - 2 : n]]
-        outs[i][0:n, :] = (smoothed[0] * smoothed[1]).astype(jnp.bfloat16)
+            edges += [ext[s, 8:16, :][0:2], ext[s, n : n + 8, :][6:8]]
         spare = outs[i].shape[0] - n - 8 - 2 * groups
         edges += tails + ([jnp.zeros((spare, lanes), jnp.float32)] if spare else [])
         outs[i][n:, :] = jnp.concatenate(edges, 0).astype(jnp.bfloat16)
@@ -334,8 +349,8 @@
                 pltpu.VMEM((len(places), 2, block_len, lanes), jnp.bfloat16),
                 pltpu.VMEM((EXTRA, channels), jnp.bfloat16),
                 pltpu.VMEM(short_taps.shape, jnp.float32),
-                pltpu.VMEM((block_len + 8, lanes), jnp.float32),
-                pltpu.SemaphoreType.DMA((len(places), 2)),
+                pltpu.VMEM((2, block_len + 8, lanes), jnp.float32),
+                pltpu.SemaphoreType.DMA((len(places), 2, 2)),
                 pltpu.SemaphoreType.DMA,
                 pltpu.SemaphoreType.DMA,
                 pltpu.SemaphoreType.DMA,

time: 47 us -> 47.1 us (level)
  no operation moved by 1% of the time
where the time goes in v1:
time: 47.1 us; the launch traced here: 46.9 us
  starting transfers between devices  19.1 us (41%)
  waiting for transfers between devices  14.6 us (31%)
  Pallas kernels  13.1 us (28%)
    ppermute x15, starting transfers between devices, swapped(): lax.ppermute(x, axis, [(i, i ^ offset) for i in range(lax.axis_size(axis))])  16.5 us
    ppermute x15, waiting for transfers between devices, swapped(): lax.ppermute(x, axis, [(i, i ^ offset) for i in range(lax.axis_size(axis))])  14.6 us
    pallas_call x2, Pallas kernels, products(): pl.pallas_call(functools.partial(product_kernel, groups, places), in_spec...  2.93 us
    ppermute x1, starting transfers between devices, turned(): return lax.ppermute(x, axis, [(i, (i + by) % peers) for i in range(peers)])  2.56 us
    pallas_call x1, Pallas kernels, spread(): pl.pallas_call(functools.partial(filter_kernel, groups), in_specs=[SMEM]...  2.36 us
    pallas_call x3, Pallas kernels, projected(): pl.pallas_call(functools.partial(project_kernel, back_offsets, own, colum...  1.85 us
    pallas_call x1, Pallas kernels, spread(): pl.pallas_call(query_kernel, in_specs=[HBM, VMEM], out_specs=[VMEM] * 2,...  1.82 us
    pallas_call x1, Pallas kernels, spread(): pl.pallas_call(functools.partial(conv_kernel, offsets, len(near)), in_spe...  1.81 us
  transfers between devices with their start and end apart: 16, of which 9 were waited for; matrix products, arithmetic and copies ran while one was open for 0% of the time, Pallas kernels for 25%

profile of v1, /device:TPU:0, one launch (start us, length us, event | category | flops | bytes accessed | tf_op | source)
XLA Modules:
  0.0 46.9 jit_solution(17637789013042165633)
XLA Ops:
  0.5 1.5 %product.2 = (bf16[128,1024]{1,0:T(8,128)(2,1)S(1)}, bf16[528,128]{1,0:T(8,128)(2,1)S(1)}, bf16[528,128]{1,0:T(8,128)(2,1)S(1)}) custom-call(bf16[3,512,512]{2,1,0:T(8,128)(2,1)} %bitcast.4, f32[3,3,512]{2,1,0:T(4,128)} %taps_ref.3, bf16[512,1024]{1,0:T(8,128)(2,1)} %refs_0_.1), custom_call_target="tpu_custom_call" | custom-call | tf_op jit(solution)/shard_map/product/pallas_call | solution.py:343
  2.0 2.6 %collective-permute-start = (bf16[128,1024]{1,0:T(8,128)(2,1)S(1)}, bf16[128,1024]{1,0:T(8,128)(2,1)S(1)}, u32[]{:S(2)}, u32[]{:S(2)}) collective-permute-start(bf16[128,1024]{1,0:T(8,128)(2,1)S(1)} %get-tuple-element.45.refs_0_), channel_id=1, source_target_pairs={{0,1},{1,0},{2,3},{3,2},{4,5},{5,4},{6,7},{7,6},{8,9},{9,8},{10,11... | collective-permute-start | bytes 786440 | tf_op jit(solution)/shard_map/ppermute | solution.py:320
  4.5 2.6 %collective-permute-start.1 = (bf16[528,128]{1,0:T(8,128)(2,1)S(1)}, bf16[528,128]{1,0:T(8,128)(2,1)S(1)}, u32[]{:S(2)}, u32[]{:S(2)}) collective-permute-start(bf16[528,128]{1,0:T(8,128)(2,1)S(1)} %get-tuple-element.49), channel_id=1, source_target_pairs={{0,16},{8,24},{16,0},{24,8},{1,17},{9,25},{17,1},{25,9},{2,18},{10... | collective-permute-start | bytes 405512 | tf_op jit(solution)/shard_map/ppermute | solution.py:311
  7.1 1.4 %collective-permute-start.2 = (bf16[528,128]{1,0:T(8,128)(2,1)S(1)}, bf16[528,128]{1,0:T(8,128)(2,1)S(1)}, u32[]{:S(2)}, u32[]{:S(2)}) collective-permute-start(bf16[528,128]{1,0:T(8,128)(2,1)S(1)} %get-tuple-element.50), channel_id=1, source_target_pairs={{0,24},{8,16},{16,8},{24,0},{1,25},{9,17},{17,9},{25,1},{2,26},{10... | collective-permute-start | bytes 405512 | tf_op jit(solution)/shard_map/ppermute | solution.py:311
  8.5 1.4 %product.3 = (bf16[528,128]{1,0:T(8,128)(2,1)S(1)}, bf16[528,128]{1,0:T(8,128)(2,1)S(1)}) custom-call(bf16[3,512,512]{2,1,0:T(8,128)(2,1)} %bitcast.5, f32[3,3,512]{2,1,0:T(4,128)} %taps_ref.3), custom_call_target="tpu_custom_call" | custom-call | tf_op jit(solution)/shard_map/product/pallas_call | solution.py:343
  10.2 1.8 %smoothed_query.1 = (f32[2,128,512]{2,1,0:T(8,128)S(1)}, bf16[2,128,512]{2,1,0:T(8,128)(2,1)S(1)}) custom-call(bf16[3,512,512]{2,1,0:T(8,128)(2,1)} %bitcast.6, f32[3,3,512]{2,1,0:T(4,128)S(1)} %copy-done.3), custom_call_target="tpu_custom_call" | custom-call | tf_op jit(solution)/shard_map/smoothed_query/pallas_call | solution.py:374
  12.1 2.4 %filter_spectra.1 = (f32[4,1024,128]{2,1,0:T(8,128)S(1)}, f32[7,16,128]{2,1,0:T(8,128)S(1)}) custom-call(s32[1,4]{1,0:T(1,128)S(1)} %copy-done.4, bf16[1024,512]{1,0:T(8,128)(2,1)S(1)} %copy-done.2, bf16[128,1024]{1,0:T(8,128)(2,1)S(1)} %get-tuple-element.45.refs_0_, bf16[128,1024]{1,0:T(8,128)(2,1)S(1)} %collective-permute-done.refs_1_), custom_call_target="tpu_custom_call" | custom-call | tf_op jit(solution)/shard_map/filter_spectra/pallas_call | solution.py:391
  14.5 3.2 %collective-permute-done.1.refs_0_ = bf16[528,128]{1,0:T(8,128)(2,1)S(1)} collective-permute-done((bf16[528,128]{1,0:T(8,128)(2,1)S(1)}, bf16[528,128]{1,0:T(8,128)(2,1)S(1)}, u32[]{:S(2)}, u32[]{:S(2)}) %collective-permute-start.1) | collective-permute-done | bytes 135200 | tf_op jit(solution)/shard_map/ppermute | solution.py:311
  17.8 1.7 %collective-permute-done.3.refs_0_ = bf16[528,128]{1,0:T(8,128)(2,1)S(1)} collective-permute-done((bf16[528,128]{1,0:T(8,128)(2,1)S(1)}, bf16[528,128]{1,0:T(8,128)(2,1)S(1)}, u32[]{:S(2)}, u32[]{:S(2)}) %collective-permute-start.3) | collective-permute-done | bytes 135200 | tf_op jit(solution)/shard_map/ppermute | solution.py:311
  19.5 1.8 %long_conv.1 = (bf16[4,144,128]{2,1,0:T(8,128)(2,1)S(1)}, bf16[4,16,128]{2,1,0:T(8,128)(2,1)S(1)}, bf16[1024,512]{1,0:T(8,128)(2,1)S(1)}, bf16[512,512]{1,0:T(8,128)(2,1)S(1)}) custom-call(f32[7,16,128]{2,1,0:T(8,128)S(1)} %get-tuple-element.51.masks_ref, bf16[512,512]{1,0:T(8,128)(2,1)S(1)} %get-tuple-element.54.far_ref, ...), custom_call_target="tpu_custom_call", output_to_operand_aliasing={{3}: (1, {})} | custom-call | tf_op jit(solution)/shard_map/long_conv/pallas_call | solution.py:417
  21.4 0.7 %long_conv_rest.1 = (bf16[4,128,128]{2,1,0:T(8,128)(2,1)S(1)}, bf16[4,128,128]{2,1,0:T(8,128)(2,1)S(1)}, bf16[4,128,128]{2,1,0:T(8,128)(2,1)S(1)}) custom-call(bf16[512,1024]{1,0:T(8,128)(2,1)S(1)} %copy-done.1, bf16[1024,512]{1,0:T(8,128)(2,1)S(1)} %get-tuple-element.59.zed_ref), custom_call_target="tpu_custom_call" | custom-call | tf_op jit(solution)/shard_map/long_conv_rest/pallas_call | solution.py:437
  22.8 3.1 %collective-permute-start.11 = (bf16[128,256]{1,0:T(8,128)(2,1)S(1)}, bf16[128,256]{1,0:T(8,128)(2,1)S(1)}, u32[]{:S(2)}, u32[]{:S(2)}) collective-permute-start(bf16[128,256]{1,0:T(8,128)(2,1)S(1)} %get-tuple-element.75), channel_id=1, source_target_pairs={{0,16},{8,24},{16,0},{24,8},{1,17},{9,25},{17,1},{25,9},{2,18},{10... | collective-permute-start | bytes 196616 | tf_op jit(solution)/shard_map/ppermute | solution.py:311
  25.9 1.0 %collective-permute-start.12 = (bf16[128,256]{1,0:T(8,128)(2,1)S(1)}, bf16[128,256]{1,0:T(8,128)(2,1)S(1)}, u32[]{:S(2)}, u32[]{:S(2)}) collective-permute-start(bf16[128,256]{1,0:T(8,128)(2,1)S(1)} %get-tuple-element.76), channel_id=1, source_target_pairs={{0,8},{8,0},{16,24},{24,16},{1,9},{9,1},{17,25},{25,17},{2,10},{10... | collective-permute-start | bytes 196616 | tf_op jit(solution)/shard_map/ppermute | solution.py:311
  27.5 2.3 %collective-permute-done.11.refs_0_ = bf16[128,256]{1,0:T(8,128)(2,1)S(1)} collective-permute-done((bf16[128,256]{1,0:T(8,128)(2,1)S(1)}, bf16[128,256]{1,0:T(8,128)(2,1)S(1)}, u32[]{:S(2)}, u32[]{:S(2)}) %collective-permute-start.11) | collective-permute-done | bytes 65568 | tf_op jit(solution)/shard_map/ppermute | solution.py:311
  29.8 0.8 %collective-permute-done.12.refs_1_ = bf16[128,256]{1,0:T(8,128)(2,1)S(1)} collective-permute-done((bf16[128,256]{1,0:T(8,128)(2,1)S(1)}, bf16[128,256]{1,0:T(8,128)(2,1)S(1)}, u32[]{:S(2)}, u32[]{:S(2)}) %collective-permute-start.12) | collective-permute-done | bytes 65568 | tf_op jit(solution)/shard_map/ppermute | solution.py:311
  30.6 2.3 %collective-permute-done.13.refs_2_ = bf16[128,256]{1,0:T(8,128)(2,1)S(1)} collective-permute-done((bf16[128,256]{1,0:T(8,128)(2,1)S(1)}, bf16[128,256]{1,0:T(8,128)(2,1)S(1)}, u32[]{:S(2)}, u32[]{:S(2)}) %collective-permute-start.13) | collective-permute-done | bytes 65568 | tf_op jit(solution)/shard_map/ppermute | solution.py:311
  33.5 1.6 %collective-permute-start.15 = (bf16[128,1024]{1,0:T(8,128)(2,1)S(1)}, bf16[128,1024]{1,0:T(8,128)(2,1)S(1)}, u32[]{:S(2)}, u32[]{:S(2)}) collective-permute-start(bf16[128,1024]{1,0:T(8,128)(2,1)S(1)} %gate_project.5), channel_id=1, source_target_pairs={{0,4},{4,0},{1,5},{5,1},{2,6},{6,2},{3,7},{7,3},{8,12},{12,8},{9,1... | collective-permute-start | bytes 786440 | tf_op jit(solution)/shard_map/ppermute | solution.py:311
  36.2 1.7 %collective-permute-start.8 = (bf16[128,256]{1,0:T(8,128)(2,1)S(1)}, bf16[128,256]{1,0:T(8,128)(2,1)S(1)}, u32[]{:S(2)}, u32[]{:S(2)}) collective-permute-start(bf16[128,256]{1,0:T(8,128)(2,1)S(1)} %get-tuple-element.70), channel_id=1, source_target_pairs={{0,16},{8,24},{16,0},{24,8},{1,17},{9,25},{17,1},{25,9},{2,18},{10... | collective-permute-start | bytes 196616 | tf_op jit(solution)/shard_map/ppermute | solution.py:311
  38.5 2.1 %collective-permute-start.10 = (bf16[128,256]{1,0:T(8,128)(2,1)S(1)}, bf16[128,256]{1,0:T(8,128)(2,1)S(1)}, u32[]{:S(2)}, u32[]{:S(2)}) collective-permute-start(bf16[128,256]{1,0:T(8,128)(2,1)S(1)} %get-tuple-element.72), channel_id=1, source_target_pairs={{0,24},{8,16},{16,8},{24,0},{1,25},{9,17},{17,9},{25,1},{2,26},{10... | collective-permute-start | bytes 196616 | tf_op jit(solution)/shard_map/ppermute | solution.py:311
  40.6 2.2 %collective-permute-done.8.refs_0_ = bf16[128,256]{1,0:T(8,128)(2,1)S(1)} collective-permute-done((bf16[128,256]{1,0:T(8,128)(2,1)S(1)}, bf16[128,256]{1,0:T(8,128)(2,1)S(1)}, u32[]{:S(2)}, u32[]{:S(2)}) %collective-permute-start.8) | collective-permute-done | bytes 65568 | tf_op jit(solution)/shard_map/ppermute | solution.py:311
  43.0 1.6 %collective-permute-done.10.refs_2_ = bf16[128,256]{1,0:T(8,128)(2,1)S(1)} collective-permute-done((bf16[128,256]{1,0:T(8,128)(2,1)S(1)}, bf16[128,256]{1,0:T(8,128)(2,1)S(1)}, u32[]{:S(2)}, u32[]{:S(2)}) %collective-permute-start.10) | collective-permute-done | bytes 65568 | tf_op jit(solution)/shard_map/ppermute | solution.py:311
  44.6 0.8 %gate_project.3.own_ref = f32[128,2048]{1,0:T(8,128)S(1)} custom-call(f32[2,128,512]{2,1,0:T(8,128)S(1)} %get-tuple-element.66.keep_ref, bf16[2,128,512]{2,1,0:T(8,128)(2,1)S(1)} %collective-permute-done.5.other_ref, bf16[4,16,128]{2,1,0:T(8,128)(2,1)S(1)} %get-tuple-element.68.added_ref, bf16[4,144,128]{2,1,0:T(8,128)(2,1)S(1)} %collective-permute-done.6.crossed_ref, ...), custom_call_target="tpu_custom_call" | custom-call | tf_op jit(solution)/shard_map/gate_project/pallas_call | solution.py:463
  45.4 0.7 %sum.2.refs_0_ = bf16[128,2048]{1,0:T(8,128)(2,1)} custom-call(f32[128,2048]{1,0:T(8,128)S(1)} %gate_project.3.own_ref, bf16[128,1024]{1,0:T(8,128)(2,1)S(1)} %collective-permute-done.15.got_ref), custom_call_target="tpu_custom_call" | custom-call | tf_op jit(solution)/shard_map/sum/pallas_call | solution.py:481
  46.2 0.7 %sum.3 = bf16[128,2048]{1,0:T(8,128)(2,1)} custom-call(f32[128,2048]{1,0:T(8,128)S(1)} %gate_project.3.own_ref, bf16[128,1024]{1,0:T(8,128)(2,1)S(1)} %collective-permute-done.14.got_ref, bf16[128,2048]{1,0:T(8,128)(2,1)} %sum.2.refs_0_), custom_call_target="tpu_custom_call", output_to_operand_aliasing={{}: (2, {})} | custom-call | tf_op jit(solution)/shard_map/sum/pallas_call | solution.py:481
  (32 shorter events, 4.7 us)
Async XLA Ops:
  0.0 33.0 %collective-permute-start.7 = (bf16[512,2048]{1,0:T(8,128)(2,1)}, bf16[512,2048]{1,0:T(8,128)(2,1)S(1)}, u32[]{:S(2)}, u32[]{:S(2)}) collective-permute-start(bf16[512,2048]{1,0:T(8,128)(2,1)} %w_ref.5), channel_id=1, source_target_pairs={{0,2},{2,0},{1,3},{3,1},{4,6},{6,4},{5,7},{7,5},{8,10},{10,8},{9,1... | collective-permute-start | bytes 6291464 | tf_op jit(solution)/shard_map/ppermute | solution.py:311
  0.5 9.7 %copy-start.3 = (f32[3,3,512]{2,1,0:T(4,128)S(1)}, f32[3,3,512]{2,1,0:T(4,128)}, u32[]{:S(2)}) copy-start(f32[3,3,512]{2,1,0:T(4,128)} %taps_ref.3) | copy-start | bytes 55300
  2.0 10.2 %copy-start.2 = (bf16[1024,512]{1,0:T(8,128)(2,1)S(1)}, bf16[1024,512]{1,0:T(8,128)(2,1)}, u32[]{:S(2)}) copy-start(bf16[1024,512]{1,0:T(8,128)(2,1)} %constant.4.clone.fwd_ref) | copy-start | bytes 3145732
  2.0 10.2 %copy-start.4 = (s32[1,4]{1,0:T(1,128)S(1)}, s32[1,4]{1,0:T(1,128)}, u32[]{:S(2)}) copy-start(s32[1,4]{1,0:T(1,128)} %begin_ref.1) | copy-start | bytes 52
  2.0 10.0 %collective-permute-start = (bf16[128,1024]{1,0:T(8,128)(2,1)S(1)}, bf16[128,1024]{1,0:T(8,128)(2,1)S(1)}, u32[]{:S(2)}, u32[]{:S(2)}) collective-permute-start(bf16[128,1024]{1,0:T(8,128)(2,1)S(1)} %get-tuple-element.45.refs_0_), channel_id=1, source_target_pairs={{0,1},{1,0},{2,3},{3,2},{4,5},{5,4},{6,7},{7,6},{8,9},{9,8},{10,11... | collective-permute-start | bytes 786440 | tf_op jit(solution)/shard_map/ppermute | solution.py:320
  4.5 13.2 %collective-permute-start.1 = (bf16[528,128]{1,0:T(8,128)(2,1)S(1)}, bf16[528,128]{1,0:T(8,128)(2,1)S(1)}, u32[]{:S(2)}, u32[]{:S(2)}) collective-permute-start(bf16[528,128]{1,0:T(8,128)(2,1)S(1)} %get-tuple-element.49), channel_id=1, source_target_pairs={{0,16},{8,24},{16,0},{24,8},{1,17},{9,25},{17,1},{25,9},{2,18},{10... | collective-permute-start | bytes 405512 | tf_op jit(solution)/shard_map/ppermute | solution.py:311
  7.1 10.6 %collective-permute-start.2 = (bf16[528,128]{1,0:T(8,128)(2,1)S(1)}, bf16[528,128]{1,0:T(8,128)(2,1)S(1)}, u32[]{:S(2)}, u32[]{:S(2)}) collective-permute-start(bf16[528,128]{1,0:T(8,128)(2,1)S(1)} %get-tuple-element.50), channel_id=1, source_target_pairs={{0,24},{8,16},{16,8},{24,0},{1,25},{9,17},{17,9},{25,1},{2,26},{10... | collective-permute-start | bytes 405512 | tf_op jit(solution)/shard_map/ppermute | solution.py:311
  9.9 9.5 %copy-start.1 = (bf16[512,1024]{1,0:T(8,128)(2,1)S(1)}, bf16[512,1024]{1,0:T(8,128)(2,1)}, u32[]{:S(2)}) copy-start(bf16[512,1024]{1,0:T(8,128)(2,1)} %constant.5.clone.inv_ref) | copy-start | bytes 3145732
  10.0 9.5 %collective-permute-start.3 = (bf16[528,128]{1,0:T(8,128)(2,1)S(1)}, bf16[528,128]{1,0:T(8,128)(2,1)S(1)}, u32[]{:S(2)}, u32[]{:S(2)}) collective-permute-start(bf16[528,128]{1,0:T(8,128)(2,1)S(1)} %get-tuple-element.57), channel_id=1, source_target_pairs={{0,8},{8,0},{16,24},{24,16},{1,9},{9,1},{17,25},{25,17},{2,10},{10... | collective-permute-start | bytes 405512 | tf_op jit(solution)/shard_map/ppermute | solution.py:311
  12.0 20.9 %collective-permute-start.5 = (bf16[2,128,512]{2,1,0:T(8,128)(2,1)S(1)}, bf16[2,128,512]{2,1,0:T(8,128)(2,1)S(1)}, u32[]{:S(2)}, u32[]{:S(2)}) collective-permute-start(bf16[2,128,512]{2,1,0:T(8,128)(2,1)S(1)} %get-tuple-element.67), channel_id=1, source_target_pairs={{0,2},{2,0},{1,3},{3,1},{4,6},{6,4},{5,7},{7,5},{8,10},{10,8},{9,1... | collective-permute-start | bytes 786440 | tf_op jit(solution)/shard_map/ppermute | solution.py:311
  21.3 11.7 %copy-start = (bf16[512,2048]{1,0:T(8,128)(2,1)S(1)}, bf16[512,2048]{1,0:T(8,128)(2,1)}, u32[]{:S(2)}) copy-start(bf16[512,2048]{1,0:T(8,128)(2,1)} %w_ref.5) | copy-start | bytes 6291460
  21.3 1.4 %collective-permute-start.6 = (bf16[4,144,128]{2,1,0:T(8,128)(2,1)S(1)}, bf16[4,144,128]{2,1,0:T(8,128)(2,1)S(1)}, u32[]{:S(2)}, u32[]{:S(2)}) collective-permute-start(bf16[4,144,128]{2,1,0:T(8,128)(2,1)S(1)} %get-tuple-element.69), channel_id=1, source_target_pairs={{0,2},{2,0},{1,3},{3,1},{4,6},{6,4},{5,7},{7,5},{8,10},{10,8},{9,1... | collective-permute-start | bytes 442376 | tf_op jit(solution)/shard_map/ppermute | solution.py:311
  22.1 4.8 %collective-permute-start.4 = (bf16[4,128,128]{2,1,0:T(8,128)(2,1)S(1)}, bf16[4,128,128]{2,1,0:T(8,128)(2,1)S(1)}, u32[]{:S(2)}, u32[]{:S(2)}) collective-permute-start(bf16[4,128,128]{2,1,0:T(8,128)(2,1)S(1)} %get-tuple-element.61), channel_id=1, source_target_pairs={{0,2},{2,0},{1,3},{3,1},{4,6},{6,4},{5,7},{7,5},{8,10},{10,8},{9,1... | collective-permute-start | bytes 393224 | tf_op jit(solution)/shard_map/ppermute | solution.py:311
  22.8 7.0 %collective-permute-start.11 = (bf16[128,256]{1,0:T(8,128)(2,1)S(1)}, bf16[128,256]{1,0:T(8,128)(2,1)S(1)}, u32[]{:S(2)}, u32[]{:S(2)}) collective-permute-start(bf16[128,256]{1,0:T(8,128)(2,1)S(1)} %get-tuple-element.75), channel_id=1, source_target_pairs={{0,16},{8,24},{16,0},{24,8},{1,17},{9,25},{17,1},{25,9},{2,18},{10... | collective-permute-start | bytes 196616 | tf_op jit(solution)/shard_map/ppermute | solution.py:311
  25.9 4.7 %collective-permute-start.12 = (bf16[128,256]{1,0:T(8,128)(2,1)S(1)}, bf16[128,256]{1,0:T(8,128)(2,1)S(1)}, u32[]{:S(2)}, u32[]{:S(2)}) collective-permute-start(bf16[128,256]{1,0:T(8,128)(2,1)S(1)} %get-tuple-element.76), channel_id=1, source_target_pairs={{0,8},{8,0},{16,24},{24,16},{1,9},{9,1},{17,25},{25,17},{2,10},{10... | collective-permute-start | bytes 196616 | tf_op jit(solution)/shard_map/ppermute | solution.py:311
  26.9 6.1 %collective-permute-start.13 = (bf16[128,256]{1,0:T(8,128)(2,1)S(1)}, bf16[128,256]{1,0:T(8,128)(2,1)S(1)}, u32[]{:S(2)}, u32[]{:S(2)}) collective-permute-start(bf16[128,256]{1,0:T(8,128)(2,1)S(1)} %get-tuple-element.77), channel_id=1, source_target_pairs={{0,24},{8,16},{16,8},{24,0},{1,25},{9,17},{17,9},{25,1},{2,26},{10... | collective-permute-start | bytes 196616 | tf_op jit(solution)/shard_map/ppermute | solution.py:311
  33.5 11.9 %collective-permute-start.15 = (bf16[128,1024]{1,0:T(8,128)(2,1)S(1)}, bf16[128,1024]{1,0:T(8,128)(2,1)S(1)}, u32[]{:S(2)}, u32[]{:S(2)}) collective-permute-start(bf16[128,1024]{1,0:T(8,128)(2,1)S(1)} %gate_project.5), channel_id=1, source_target_pairs={{0,4},{4,0},{1,5},{5,1},{2,6},{6,2},{3,7},{7,3},{8,12},{12,8},{9,1... | collective-permute-start | bytes 786440 | tf_op jit(solution)/shard_map/ppermute | solution.py:311
  35.6 10.5 %collective-permute-start.14 = (bf16[128,1024]{1,0:T(8,128)(2,1)S(1)}, bf16[128,1024]{1,0:T(8,128)(2,1)S(1)}, u32[]{:S(2)}, u32[]{:S(2)}) collective-permute-start(bf16[128,1024]{1,0:T(8,128)(2,1)S(1)} %gate_project.4), channel_id=1, source_target_pairs={{0,4},{4,0},{1,5},{5,1},{2,6},{6,2},{3,7},{7,3},{8,12},{12,8},{9,1... | collective-permute-start | bytes 786440 | tf_op jit(solution)/shard_map/ppermute | solution.py:311
  36.2 6.6 %collective-permute-start.8 = (bf16[128,256]{1,0:T(8,128)(2,1)S(1)}, bf16[128,256]{1,0:T(8,128)(2,1)S(1)}, u32[]{:S(2)}, u32[]{:S(2)}) collective-permute-start(bf16[128,256]{1,0:T(8,128)(2,1)S(1)} %get-tuple-element.70), channel_id=1, source_target_pairs={{0,16},{8,24},{16,0},{24,8},{1,17},{9,25},{17,1},{25,9},{2,18},{10... | collective-permute-start | bytes 196616 | tf_op jit(solution)/shard_map/ppermute | solution.py:311
  37.9 5.1 %collective-permute-start.9 = (bf16[128,256]{1,0:T(8,128)(2,1)S(1)}, bf16[128,256]{1,0:T(8,128)(2,1)S(1)}, u32[]{:S(2)}, u32[]{:S(2)}) collective-permute-start(bf16[128,256]{1,0:T(8,128)(2,1)S(1)} %get-tuple-element.71), channel_id=1, source_target_pairs={{0,8},{8,0},{16,24},{24,16},{1,9},{9,1},{17,25},{25,17},{2,10},{10... | collective-permute-start | bytes 196616 | tf_op jit(solution)/shard_map/ppermute | solution.py:311
  38.5 6.1 %collective-permute-start.10 = (bf16[128,256]{1,0:T(8,128)(2,1)S(1)}, bf16[128,256]{1,0:T(8,128)(2,1)S(1)}, u32[]{:S(2)}, u32[]{:S(2)}) collective-permute-start(bf16[128,256]{1,0:T(8,128)(2,1)S(1)} %get-tuple-element.72), channel_id=1, source_target_pairs={{0,24},{8,16},{16,8},{24,0},{1,25},{9,17},{17,9},{25,1},{2,26},{10... | collective-permute-start | bytes 196616 | tf_op jit(solution)/shard_map/ppermute | solution.py:311

commit v2 on v0

--- a/solution.py
+++ b/solution.py
@@ -460,7 +460,7 @@
     halves = [slice(at, at + width) for at in range(0, dout, width)]
     gots = [swapped(projected(False, columns, backs, jnp.bfloat16), "cy", 1) for columns in halves]
     own = projected(True, slice(0, dout), exchanged(back_offsets, second), jnp.float32)
-    steps = 4
+    steps = 2
     total = ()
     for columns, got in zip(halves, gots):
         total = pl.pallas_call(

time: 47 us -> 47 us (level)
  no operation moved by 1% of the time
where the time goes in v2:
time: 47 us; the launch traced here: 46.9 us
  starting transfers between devices  19.2 us (41%)
  waiting for transfers between devices  14.6 us (31%)
  Pallas kernels  12.9 us (27%)
    ppermute x15, starting transfers between devices, swapped(): lax.ppermute(x, axis, [(i, i ^ offset) for i in range(lax.axis_size(axis))])  16.6 us
    ppermute x15, waiting for transfers between devices, swapped(): lax.ppermute(x, axis, [(i, i ^ offset) for i in range(lax.axis_size(axis))])  14.6 us
    pallas_call x2, Pallas kernels, products(): pl.pallas_call(functools.partial(product_kernel, groups, places), in_spec...  2.83 us
    ppermute x1, starting transfers between devices, turned(): return lax.ppermute(x, axis, [(i, (i + by) % peers) for i in range(peers)])  2.55 us
    pallas_call x1, Pallas kernels, spread(): pl.pallas_call(functools.partial(filter_kernel, groups), in_specs=[SMEM]...  2.37 us
    pallas_call x3, Pallas kernels, projected(): pl.pallas_call(functools.partial(project_kernel, back_offsets, own, colum...  1.84 us
    pallas_call x1, Pallas kernels, spread(): pl.pallas_call(functools.partial(conv_kernel, offsets, len(near)), in_spe...  1.81 us
    pallas_call x1, Pallas kernels, spread(): pl.pallas_call(query_kernel, in_specs=[HBM, VMEM], out_specs=[VMEM] * 2,...  1.78 us
  transfers between devices with their start and end apart: 16, of which 9 were waited for; matrix products, arithmetic and copies ran while one was open for 0% of the time, Pallas kernels for 25%

profile of v2, /device:TPU:0, one launch (start us, length us, event | category | flops | bytes accessed | tf_op | source)
XLA Modules:
  0.0 46.9 jit_solution(4877741580544065403)
XLA Ops:
  0.5 1.4 %product.2 = (bf16[128,1024]{1,0:T(8,128)(2,1)S(1)}, bf16[528,128]{1,0:T(8,128)(2,1)S(1)}, bf16[528,128]{1,0:T(8,128)(2,1)S(1)}) custom-call(bf16[3,512,512]{2,1,0:T(8,128)(2,1)} %bitcast.4, f32[3,3,512]{2,1,0:T(4,128)} %taps_ref.3, bf16[512,1024]{1,0:T(8,128)(2,1)} %refs_0_.1), custom_call_target="tpu_custom_call" | custom-call | tf_op jit(solution)/shard_map/product/pallas_call | solution.py:328
  1.9 2.6 %collective-permute-start = (bf16[128,1024]{1,0:T(8,128)(2,1)S(1)}, bf16[128,1024]{1,0:T(8,128)(2,1)S(1)}, u32[]{:S(2)}, u32[]{:S(2)}) collective-permute-start(bf16[128,1024]{1,0:T(8,128)(2,1)S(1)} %get-tuple-element.45.refs_0_), channel_id=1, source_target_pairs={{0,1},{1,0},{2,3},{3,2},{4,5},{5,4},{6,7},{7,6},{8,9},{9,8},{10,11... | collective-permute-start | bytes 786440 | tf_op jit(solution)/shard_map/ppermute | solution.py:305
  4.5 2.6 %collective-permute-start.1 = (bf16[528,128]{1,0:T(8,128)(2,1)S(1)}, bf16[528,128]{1,0:T(8,128)(2,1)S(1)}, u32[]{:S(2)}, u32[]{:S(2)}) collective-permute-start(bf16[528,128]{1,0:T(8,128)(2,1)S(1)} %get-tuple-element.49), channel_id=1, source_target_pairs={{0,16},{8,24},{16,0},{24,8},{1,17},{9,25},{17,1},{25,9},{2,18},{10... | collective-permute-start | bytes 405512 | tf_op jit(solution)/shard_map/ppermute | solution.py:296
  7.1 1.4 %collective-permute-start.2 = (bf16[528,128]{1,0:T(8,128)(2,1)S(1)}, bf16[528,128]{1,0:T(8,128)(2,1)S(1)}, u32[]{:S(2)}, u32[]{:S(2)}) collective-permute-start(bf16[528,128]{1,0:T(8,128)(2,1)S(1)} %get-tuple-element.50), channel_id=1, source_target_pairs={{0,24},{8,16},{16,8},{24,0},{1,25},{9,17},{17,9},{25,1},{2,26},{10... | collective-permute-start | bytes 405512 | tf_op jit(solution)/shard_map/ppermute | solution.py:296
  8.4 1.4 %product.3 = (bf16[528,128]{1,0:T(8,128)(2,1)S(1)}, bf16[528,128]{1,0:T(8,128)(2,1)S(1)}) custom-call(bf16[3,512,512]{2,1,0:T(8,128)(2,1)} %bitcast.5, f32[3,3,512]{2,1,0:T(4,128)} %taps_ref.3), custom_call_target="tpu_custom_call" | custom-call | tf_op jit(solution)/shard_map/product/pallas_call | solution.py:328
  10.1 1.8 %smoothed_query.1 = (f32[2,128,512]{2,1,0:T(8,128)S(1)}, bf16[2,128,512]{2,1,0:T(8,128)(2,1)S(1)}) custom-call(bf16[3,512,512]{2,1,0:T(8,128)(2,1)} %bitcast.6, f32[3,3,512]{2,1,0:T(4,128)S(1)} %copy-done.3), custom_call_target="tpu_custom_call" | custom-call | tf_op jit(solution)/shard_map/smoothed_query/pallas_call | solution.py:359
  12.0 2.4 %filter_spectra.1 = (f32[4,1024,128]{2,1,0:T(8,128)S(1)}, f32[7,16,128]{2,1,0:T(8,128)S(1)}) custom-call(s32[1,4]{1,0:T(1,128)S(1)} %copy-done.4, bf16[1024,512]{1,0:T(8,128)(2,1)S(1)} %copy-done.2, bf16[128,1024]{1,0:T(8,128)(2,1)S(1)} %get-tuple-element.45.refs_0_, bf16[128,1024]{1,0:T(8,128)(2,1)S(1)} %collective-permute-done.refs_1_), custom_call_target="tpu_custom_call" | custom-call | tf_op jit(solution)/shard_map/filter_spectra/pallas_call | solution.py:376
  14.4 3.2 %collective-permute-done.1.refs_0_ = bf16[528,128]{1,0:T(8,128)(2,1)S(1)} collective-permute-done((bf16[528,128]{1,0:T(8,128)(2,1)S(1)}, bf16[528,128]{1,0:T(8,128)(2,1)S(1)}, u32[]{:S(2)}, u32[]{:S(2)}) %collective-permute-start.1) | collective-permute-done | bytes 135200 | tf_op jit(solution)/shard_map/ppermute | solution.py:296
  17.7 1.7 %collective-permute-done.3.refs_0_ = bf16[528,128]{1,0:T(8,128)(2,1)S(1)} collective-permute-done((bf16[528,128]{1,0:T(8,128)(2,1)S(1)}, bf16[528,128]{1,0:T(8,128)(2,1)S(1)}, u32[]{:S(2)}, u32[]{:S(2)}) %collective-permute-start.3) | collective-permute-done | bytes 135200 | tf_op jit(solution)/shard_map/ppermute | solution.py:296
  19.4 1.8 %long_conv.1 = (bf16[4,144,128]{2,1,0:T(8,128)(2,1)S(1)}, bf16[4,16,128]{2,1,0:T(8,128)(2,1)S(1)}, bf16[1024,512]{1,0:T(8,128)(2,1)S(1)}, bf16[512,512]{1,0:T(8,128)(2,1)S(1)}) custom-call(f32[7,16,128]{2,1,0:T(8,128)S(1)} %get-tuple-element.51.masks_ref, bf16[512,512]{1,0:T(8,128)(2,1)S(1)} %get-tuple-element.54.far_ref, ...), custom_call_target="tpu_custom_call", output_to_operand_aliasing={{3}: (1, {})} | custom-call | tf_op jit(solution)/shard_map/long_conv/pallas_call | solution.py:402
  21.3 0.7 %long_conv_rest.1 = (bf16[4,128,128]{2,1,0:T(8,128)(2,1)S(1)}, bf16[4,128,128]{2,1,0:T(8,128)(2,1)S(1)}, bf16[4,128,128]{2,1,0:T(8,128)(2,1)S(1)}) custom-call(bf16[512,1024]{1,0:T(8,128)(2,1)S(1)} %copy-done.1, bf16[1024,512]{1,0:T(8,128)(2,1)S(1)} %get-tuple-element.59.zed_ref), custom_call_target="tpu_custom_call" | custom-call | tf_op jit(solution)/shard_map/long_conv_rest/pallas_call | solution.py:422
  22.7 3.1 %collective-permute-start.11 = (bf16[128,256]{1,0:T(8,128)(2,1)S(1)}, bf16[128,256]{1,0:T(8,128)(2,1)S(1)}, u32[]{:S(2)}, u32[]{:S(2)}) collective-permute-start(bf16[128,256]{1,0:T(8,128)(2,1)S(1)} %get-tuple-element.75), channel_id=1, source_target_pairs={{0,16},{8,24},{16,0},{24,8},{1,17},{9,25},{17,1},{25,9},{2,18},{10... | collective-permute-start | bytes 196616 | tf_op jit(solution)/shard_map/ppermute | solution.py:296
  25.9 1.0 %collective-permute-start.12 = (bf16[128,256]{1,0:T(8,128)(2,1)S(1)}, bf16[128,256]{1,0:T(8,128)(2,1)S(1)}, u32[]{:S(2)}, u32[]{:S(2)}) collective-permute-start(bf16[128,256]{1,0:T(8,128)(2,1)S(1)} %get-tuple-element.76), channel_id=1, source_target_pairs={{0,8},{8,0},{16,24},{24,16},{1,9},{9,1},{17,25},{25,17},{2,10},{10... | collective-permute-start | bytes 196616 | tf_op jit(solution)/shard_map/ppermute | solution.py:296
  27.5 2.3 %collective-permute-done.11.refs_0_ = bf16[128,256]{1,0:T(8,128)(2,1)S(1)} collective-permute-done((bf16[128,256]{1,0:T(8,128)(2,1)S(1)}, bf16[128,256]{1,0:T(8,128)(2,1)S(1)}, u32[]{:S(2)}, u32[]{:S(2)}) %collective-permute-start.11) | collective-permute-done | bytes 65568 | tf_op jit(solution)/shard_map/ppermute | solution.py:296
  29.8 0.8 %collective-permute-done.12.refs_1_ = bf16[128,256]{1,0:T(8,128)(2,1)S(1)} collective-permute-done((bf16[128,256]{1,0:T(8,128)(2,1)S(1)}, bf16[128,256]{1,0:T(8,128)(2,1)S(1)}, u32[]{:S(2)}, u32[]{:S(2)}) %collective-permute-start.12) | collective-permute-done | bytes 65568 | tf_op jit(solution)/shard_map/ppermute | solution.py:296
  30.6 2.3 %collective-permute-done.13.refs_2_ = bf16[128,256]{1,0:T(8,128)(2,1)S(1)} collective-permute-done((bf16[128,256]{1,0:T(8,128)(2,1)S(1)}, bf16[128,256]{1,0:T(8,128)(2,1)S(1)}, u32[]{:S(2)}, u32[]{:S(2)}) %collective-permute-start.13) | collective-permute-done | bytes 65568 | tf_op jit(solution)/shard_map/ppermute | solution.py:296
  33.5 1.6 %collective-permute-start.15 = (bf16[128,1024]{1,0:T(8,128)(2,1)S(1)}, bf16[128,1024]{1,0:T(8,128)(2,1)S(1)}, u32[]{:S(2)}, u32[]{:S(2)}) collective-permute-start(bf16[128,1024]{1,0:T(8,128)(2,1)S(1)} %gate_project.5), channel_id=1, source_target_pairs={{0,4},{4,0},{1,5},{5,1},{2,6},{6,2},{3,7},{7,3},{8,12},{12,8},{9,1... | collective-permute-start | bytes 786440 | tf_op jit(solution)/shard_map/ppermute | solution.py:296
  36.2 1.7 %collective-permute-start.8 = (bf16[128,256]{1,0:T(8,128)(2,1)S(1)}, bf16[128,256]{1,0:T(8,128)(2,1)S(1)}, u32[]{:S(2)}, u32[]{:S(2)}) collective-permute-start(bf16[128,256]{1,0:T(8,128)(2,1)S(1)} %get-tuple-element.70), channel_id=1, source_target_pairs={{0,16},{8,24},{16,0},{24,8},{1,17},{9,25},{17,1},{25,9},{2,18},{10... | collective-permute-start | bytes 196616 | tf_op jit(solution)/shard_map/ppermute | solution.py:296
  38.5 2.1 %collective-permute-start.10 = (bf16[128,256]{1,0:T(8,128)(2,1)S(1)}, bf16[128,256]{1,0:T(8,128)(2,1)S(1)}, u32[]{:S(2)}, u32[]{:S(2)}) collective-permute-start(bf16[128,256]{1,0:T(8,128)(2,1)S(1)} %get-tuple-element.72), channel_id=1, source_target_pairs={{0,24},{8,16},{16,8},{24,0},{1,25},{9,17},{17,9},{25,1},{2,26},{10... | collective-permute-start | bytes 196616 | tf_op jit(solution)/shard_map/ppermute | solution.py:296
  40.5 2.2 %collective-permute-done.8.refs_0_ = bf16[128,256]{1,0:T(8,128)(2,1)S(1)} collective-permute-done((bf16[128,256]{1,0:T(8,128)(2,1)S(1)}, bf16[128,256]{1,0:T(8,128)(2,1)S(1)}, u32[]{:S(2)}, u32[]{:S(2)}) %collective-permute-start.8) | collective-permute-done | bytes 65568 | tf_op jit(solution)/shard_map/ppermute | solution.py:296
  42.9 1.6 %collective-permute-done.10.refs_2_ = bf16[128,256]{1,0:T(8,128)(2,1)S(1)} collective-permute-done((bf16[128,256]{1,0:T(8,128)(2,1)S(1)}, bf16[128,256]{1,0:T(8,128)(2,1)S(1)}, u32[]{:S(2)}, u32[]{:S(2)}) %collective-permute-start.10) | collective-permute-done | bytes 65568 | tf_op jit(solution)/shard_map/ppermute | solution.py:296
  44.6 0.8 %gate_project.3.own_ref = f32[128,2048]{1,0:T(8,128)S(1)} custom-call(f32[2,128,512]{2,1,0:T(8,128)S(1)} %get-tuple-element.66.keep_ref, bf16[2,128,512]{2,1,0:T(8,128)(2,1)S(1)} %collective-permute-done.5.other_ref, bf16[4,16,128]{2,1,0:T(8,128)(2,1)S(1)} %get-tuple-element.68.added_ref, bf16[4,144,128]{2,1,0:T(8,128)(2,1)S(1)} %collective-permute-done.6.crossed_ref, ...), custom_call_target="tpu_custom_call" | custom-call | tf_op jit(solution)/shard_map/gate_project/pallas_call | solution.py:448
  45.4 0.7 %sum.2.refs_0_ = bf16[128,2048]{1,0:T(8,128)(2,1)} custom-call(f32[128,2048]{1,0:T(8,128)S(1)} %gate_project.3.own_ref, bf16[128,1024]{1,0:T(8,128)(2,1)S(1)} %collective-permute-done.15.got_ref), custom_call_target="tpu_custom_call" | custom-call | tf_op jit(solution)/shard_map/sum/pallas_call | solution.py:466
  46.1 0.7 %sum.3 = bf16[128,2048]{1,0:T(8,128)(2,1)} custom-call(f32[128,2048]{1,0:T(8,128)S(1)} %gate_project.3.own_ref, bf16[128,1024]{1,0:T(8,128)(2,1)S(1)} %collective-permute-done.14.got_ref, bf16[128,2048]{1,0:T(8,128)(2,1)} %sum.2.refs_0_), custom_call_target="tpu_custom_call", output_to_operand_aliasing={{}: (2, {})} | custom-call | tf_op jit(solution)/shard_map/sum/pallas_call | solution.py:466
  (32 shorter events, 4.8 us)
Async XLA Ops:
  0.0 32.9 %collective-permute-start.7 = (bf16[512,2048]{1,0:T(8,128)(2,1)}, bf16[512,2048]{1,0:T(8,128)(2,1)S(1)}, u32[]{:S(2)}, u32[]{:S(2)}) collective-permute-start(bf16[512,2048]{1,0:T(8,128)(2,1)} %w_ref.5), channel_id=1, source_target_pairs={{0,2},{2,0},{1,3},{3,1},{4,6},{6,4},{5,7},{7,5},{8,10},{10,8},{9,1... | collective-permute-start | bytes 6291464 | tf_op jit(solution)/shard_map/ppermute | solution.py:296
  0.5 9.7 %copy-start.3 = (f32[3,3,512]{2,1,0:T(4,128)S(1)}, f32[3,3,512]{2,1,0:T(4,128)}, u32[]{:S(2)}) copy-start(f32[3,3,512]{2,1,0:T(4,128)} %taps_ref.3) | copy-start | bytes 55300
  1.9 10.1 %copy-start.2 = (bf16[1024,512]{1,0:T(8,128)(2,1)S(1)}, bf16[1024,512]{1,0:T(8,128)(2,1)}, u32[]{:S(2)}) copy-start(bf16[1024,512]{1,0:T(8,128)(2,1)} %constant.4.clone.fwd_ref) | copy-start | bytes 3145732
  1.9 10.1 %copy-start.4 = (s32[1,4]{1,0:T(1,128)S(1)}, s32[1,4]{1,0:T(1,128)}, u32[]{:S(2)}) copy-start(s32[1,4]{1,0:T(1,128)} %begin_ref.1) | copy-start | bytes 52
  1.9 10.0 %collective-permute-start = (bf16[128,1024]{1,0:T(8,128)(2,1)S(1)}, bf16[128,1024]{1,0:T(8,128)(2,1)S(1)}, u32[]{:S(2)}, u32[]{:S(2)}) collective-permute-start(bf16[128,1024]{1,0:T(8,128)(2,1)S(1)} %get-tuple-element.45.refs_0_), channel_id=1, source_target_pairs={{0,1},{1,0},{2,3},{3,2},{4,5},{5,4},{6,7},{7,6},{8,9},{9,8},{10,11... | collective-permute-start | bytes 786440 | tf_op jit(solution)/shard_map/ppermute | solution.py:305
  4.5 13.2 %collective-permute-start.1 = (bf16[528,128]{1,0:T(8,128)(2,1)S(1)}, bf16[528,128]{1,0:T(8,128)(2,1)S(1)}, u32[]{:S(2)}, u32[]{:S(2)}) collective-permute-start(bf16[528,128]{1,0:T(8,128)(2,1)S(1)} %get-tuple-element.49), channel_id=1, source_target_pairs={{0,16},{8,24},{16,0},{24,8},{1,17},{9,25},{17,1},{25,9},{2,18},{10... | collective-permute-start | bytes 405512 | tf_op jit(solution)/shard_map/ppermute | solution.py:296
  7.1 10.6 %collective-permute-start.2 = (bf16[528,128]{1,0:T(8,128)(2,1)S(1)}, bf16[528,128]{1,0:T(8,128)(2,1)S(1)}, u32[]{:S(2)}, u32[]{:S(2)}) collective-permute-start(bf16[528,128]{1,0:T(8,128)(2,1)S(1)} %get-tuple-element.50), channel_id=1, source_target_pairs={{0,24},{8,16},{16,8},{24,0},{1,25},{9,17},{17,9},{25,1},{2,26},{10... | collective-permute-start | bytes 405512 | tf_op jit(solution)/shard_map/ppermute | solution.py:296
  9.8 9.6 %copy-start.1 = (bf16[512,1024]{1,0:T(8,128)(2,1)S(1)}, bf16[512,1024]{1,0:T(8,128)(2,1)}, u32[]{:S(2)}) copy-start(bf16[512,1024]{1,0:T(8,128)(2,1)} %constant.5.clone.inv_ref) | copy-start | bytes 3145732
  9.8 9.6 %collective-permute-start.3 = (bf16[528,128]{1,0:T(8,128)(2,1)S(1)}, bf16[528,128]{1,0:T(8,128)(2,1)S(1)}, u32[]{:S(2)}, u32[]{:S(2)}) collective-permute-start(bf16[528,128]{1,0:T(8,128)(2,1)S(1)} %get-tuple-element.57), channel_id=1, source_target_pairs={{0,8},{8,0},{16,24},{24,16},{1,9},{9,1},{17,25},{25,17},{2,10},{10... | collective-permute-start | bytes 405512 | tf_op jit(solution)/shard_map/ppermute | solution.py:296
  11.9 21.0 %collective-permute-start.5 = (bf16[2,128,512]{2,1,0:T(8,128)(2,1)S(1)}, bf16[2,128,512]{2,1,0:T(8,128)(2,1)S(1)}, u32[]{:S(2)}, u32[]{:S(2)}) collective-permute-start(bf16[2,128,512]{2,1,0:T(8,128)(2,1)S(1)} %get-tuple-element.67), channel_id=1, source_target_pairs={{0,2},{2,0},{1,3},{3,1},{4,6},{6,4},{5,7},{7,5},{8,10},{10,8},{9,1... | collective-permute-start | bytes 786440 | tf_op jit(solution)/shard_map/ppermute | solution.py:296
  21.2 11.7 %copy-start = (bf16[512,2048]{1,0:T(8,128)(2,1)S(1)}, bf16[512,2048]{1,0:T(8,128)(2,1)}, u32[]{:S(2)}) copy-start(bf16[512,2048]{1,0:T(8,128)(2,1)} %w_ref.5) | copy-start | bytes 6291460
  21.2 1.4 %collective-permute-start.6 = (bf16[4,144,128]{2,1,0:T(8,128)(2,1)S(1)}, bf16[4,144,128]{2,1,0:T(8,128)(2,1)S(1)}, u32[]{:S(2)}, u32[]{:S(2)}) collective-permute-start(bf16[4,144,128]{2,1,0:T(8,128)(2,1)S(1)} %get-tuple-element.69), channel_id=1, source_target_pairs={{0,2},{2,0},{1,3},{3,1},{4,6},{6,4},{5,7},{7,5},{8,10},{10,8},{9,1... | collective-permute-start | bytes 442376 | tf_op jit(solution)/shard_map/ppermute | solution.py:296
  22.0 4.9 %collective-permute-start.4 = (bf16[4,128,128]{2,1,0:T(8,128)(2,1)S(1)}, bf16[4,128,128]{2,1,0:T(8,128)(2,1)S(1)}, u32[]{:S(2)}, u32[]{:S(2)}) collective-permute-start(bf16[4,128,128]{2,1,0:T(8,128)(2,1)S(1)} %get-tuple-element.61), channel_id=1, source_target_pairs={{0,2},{2,0},{1,3},{3,1},{4,6},{6,4},{5,7},{7,5},{8,10},{10,8},{9,1... | collective-permute-start | bytes 393224 | tf_op jit(solution)/shard_map/ppermute | solution.py:296
  22.7 7.1 %collective-permute-start.11 = (bf16[128,256]{1,0:T(8,128)(2,1)S(1)}, bf16[128,256]{1,0:T(8,128)(2,1)S(1)}, u32[]{:S(2)}, u32[]{:S(2)}) collective-permute-start(bf16[128,256]{1,0:T(8,128)(2,1)S(1)} %get-tuple-element.75), channel_id=1, source_target_pairs={{0,16},{8,24},{16,0},{24,8},{1,17},{9,25},{17,1},{25,9},{2,18},{10... | collective-permute-start | bytes 196616 | tf_op jit(solution)/shard_map/ppermute | solution.py:296
  25.9 4.8 %collective-permute-start.12 = (bf16[128,256]{1,0:T(8,128)(2,1)S(1)}, bf16[128,256]{1,0:T(8,128)(2,1)S(1)}, u32[]{:S(2)}, u32[]{:S(2)}) collective-permute-start(bf16[128,256]{1,0:T(8,128)(2,1)S(1)} %get-tuple-element.76), channel_id=1, source_target_pairs={{0,8},{8,0},{16,24},{24,16},{1,9},{9,1},{17,25},{25,17},{2,10},{10... | collective-permute-start | bytes 196616 | tf_op jit(solution)/shard_map/ppermute | solution.py:296
  26.8 6.1 %collective-permute-start.13 = (bf16[128,256]{1,0:T(8,128)(2,1)S(1)}, bf16[128,256]{1,0:T(8,128)(2,1)S(1)}, u32[]{:S(2)}, u32[]{:S(2)}) collective-permute-start(bf16[128,256]{1,0:T(8,128)(2,1)S(1)} %get-tuple-element.77), channel_id=1, source_target_pairs={{0,24},{8,16},{16,8},{24,0},{1,25},{9,17},{17,9},{25,1},{2,26},{10... | collective-permute-start | bytes 196616 | tf_op jit(solution)/shard_map/ppermute | solution.py:296
  33.5 11.9 %collective-permute-start.15 = (bf16[128,1024]{1,0:T(8,128)(2,1)S(1)}, bf16[128,1024]{1,0:T(8,128)(2,1)S(1)}, u32[]{:S(2)}, u32[]{:S(2)}) collective-permute-start(bf16[128,1024]{1,0:T(8,128)(2,1)S(1)} %gate_project.5), channel_id=1, source_target_pairs={{0,4},{4,0},{1,5},{5,1},{2,6},{6,2},{3,7},{7,3},{8,12},{12,8},{9,1... | collective-permute-start | bytes 786440 | tf_op jit(solution)/shard_map/ppermute | solution.py:296
  35.6 10.5 %collective-permute-start.14 = (bf16[128,1024]{1,0:T(8,128)(2,1)S(1)}, bf16[128,1024]{1,0:T(8,128)(2,1)S(1)}, u32[]{:S(2)}, u32[]{:S(2)}) collective-permute-start(bf16[128,1024]{1,0:T(8,128)(2,1)S(1)} %gate_project.4), channel_id=1, source_target_pairs={{0,4},{4,0},{1,5},{5,1},{2,6},{6,2},{3,7},{7,3},{8,12},{12,8},{9,1... | collective-permute-start | bytes 786440 | tf_op jit(solution)/shard_map/ppermute | solution.py:296
  36.2 6.6 %collective-permute-start.8 = (bf16[128,256]{1,0:T(8,128)(2,1)S(1)}, bf16[128,256]{1,0:T(8,128)(2,1)S(1)}, u32[]{:S(2)}, u32[]{:S(2)}) collective-permute-start(bf16[128,256]{1,0:T(8,128)(2,1)S(1)} %get-tuple-element.70), channel_id=1, source_target_pairs={{0,16},{8,24},{16,0},{24,8},{1,17},{9,25},{17,1},{25,9},{2,18},{10... | collective-permute-start | bytes 196616 | tf_op jit(solution)/shard_map/ppermute | solution.py:296
  37.9 5.1 %collective-permute-start.9 = (bf16[128,256]{1,0:T(8,128)(2,1)S(1)}, bf16[128,256]{1,0:T(8,128)(2,1)S(1)}, u32[]{:S(2)}, u32[]{:S(2)}) collective-permute-start(bf16[128,256]{1,0:T(8,128)(2,1)S(1)} %get-tuple-element.71), channel_id=1, source_target_pairs={{0,8},{8,0},{16,24},{24,16},{1,9},{9,1},{17,25},{25,17},{2,10},{10... | collective-permute-start | bytes 196616 | tf_op jit(solution)/shard_map/ppermute | solution.py:296
  38.5 6.1 %collective-permute-start.10 = (bf16[128,256]{1,0:T(8,128)(2,1)S(1)}, bf16[128,256]{1,0:T(8,128)(2,1)S(1)}, u32[]{:S(2)}, u32[]{:S(2)}) collective-permute-start(bf16[128,256]{1,0:T(8,128)(2,1)S(1)} %get-tuple-element.72), channel_id=1, source_target_pairs={{0,24},{8,16},{16,8},{24,0},{1,25},{9,17},{17,9},{25,1},{2,26},{10... | collective-permute-start | bytes 196616 | tf_op jit(solution)/shard_map/ppermute | solution.py:296
